TPU v7x, 256 devices: a whole 4x4x8 slice. The times are simulated.
256 devices in a mesh: lat: 4 (over x_hi, core), lon: 16 (over z, x_lo), rep: 4 (over y).
Axes of the slice: x: 4 (x_hi: 2, x_lo: 2; x = x_hi * 2 + x_lo), y: 4, z: 8, core: 2. Of those that a mesh axis runs over, the one named last changes fastest.
Arguments:
- tokens: bfloat16 [4, 48, 192, 1024], P('rep', 'lat', 'lon'), may hold values from -6 to 6
- grad_out: bfloat16 [4, 48, 192, 1024], P('rep', 'lat', 'lon'), may hold values from -6 to 6
- first_gain: float32 [1024], replicated, may hold values from 0.5 to 1.5
- first_qkv_weight: bfloat16 [1024, 3072], P(('lat', 'lon')), may hold values from -0.1875 to 0.1875
- first_out_weight: bfloat16 [1024, 1024], P(('lat', 'lon')), may hold values from -0.1875 to 0.1875
- first_bias: float32 [529, 16], replicated, may hold values from -300 to 300
- second_gain: float32 [1024], replicated, may hold values from 0.5 to 1.5
- second_qkv_weight: bfloat16 [1024, 3072], P(('lat', 'lon')), may hold values from -0.1875 to 0.1875
- second_out_weight: bfloat16 [1024, 1024], P(('lat', 'lon')), may hold values from -0.1875 to 0.1875
- second_bias: float32 [529, 16], replicated, may hold values from -300 to 300
- rel_index: int32 [144, 144], replicated, may hold values from 0 to 528, as said below
- classes: int32 [48, 192], P('lat', 'lon'), may hold values from 0 to 3, as said below
Outputs:
- token_grad: bfloat16 [4, 48, 192, 1024], P('rep', 'lat', 'lon')
- first_out_grad: float32 [1024, 1024], P(('lat', 'lon'))
- second_out_grad: float32 [1024, 1024], P(('lat', 'lon'))
Inputs may be any that keep to these rules, and one draw needn't show every extreme that they name: rel_index[i, j] depends only on the offset between window positions i and j, and distinct offsets name distinct table entries. `classes`: tokens in the last 6 latitude rows of the shifted grid, which came round from the other pole, have class 2 or 3; all others 0 or 1.
All inputs are finite; a program needn't handle non-finite values.
Results may differ from a plain program's by a relative error of at most 0.022.
Values may be sent and summed in bfloat16 or wider, within the bound.
A program may use at most 128 MiB of HBM per device.

v0:
```python
import jax
import jax.numpy as jnp
from jax import lax
from jax.sharding import PartitionSpec as P

HEADS = 16
WIN = 12


EPSILON = 1e-05


def passed_along(block, axis, distance):
    devices = range(lax.axis_size(axis))
    route = [((i - distance) % len(devices), i) for i in devices]
    return lax.ppermute(block, axis, route)


def layer_norm(inputs, gains):
    values = inputs.astype(jnp.float32)
    centered = values - jnp.mean(values, axis=-1, keepdims=True)
    spread = jnp.mean(centered * centered, axis=-1, keepdims=True)
    return (centered * lax.rsqrt(spread + EPSILON) * gains).astype(jnp.bfloat16)


def to_windows(tensor):
    leading, height, breadth, features = tensor.shape
    blocks = tensor.reshape(leading, height // WIN, WIN, breadth // WIN, WIN, features)
    return blocks.transpose(0, 1, 3, 2, 4, 5).reshape(-1, WIN * WIN, features)


def from_windows(blocks, leading, height, breadth):
    features = blocks.shape[-1]
    tensor = blocks.reshape(leading, height // WIN, breadth // WIN, WIN, WIN, features)
    return tensor.transpose(0, 1, 3, 2, 4, 5).reshape(leading, height, breadth, features)


def window_attention(projected, bias_table, rel_index, classes):
    leading, height, breadth, triple = projected.shape
    features = triple // 3
    head_dim = features // HEADS
    blocks = to_windows(projected)
    windows, positions = (blocks.shape[0], blocks.shape[1])
    pieces = blocks.reshape(windows, positions, 3, HEADS, head_dim)
    query_part, key_part, value_part = (pieces[:, :, 0], pieces[:, :, 1], pieces[:, :, 2])
    scores = jnp.einsum(
        "wqhc,wkhc->whqk", query_part, key_part, preferred_element_type=jnp.float32
    ) * head_dim ** (-0.5)
    scores = scores + jnp.transpose(bias_table)[:, rel_index][None]
    if classes is not None:
        spread_classes = classes[None, :, :, None]
        labels = to_windows(spread_classes)[:, :, 0]
        matching = labels[:, :, None] == labels[:, None, :]
        scores = jnp.where(matching[:, None], scores, -jnp.inf)
    weights = jax.nn.softmax(scores, axis=-1).astype(jnp.bfloat16)
    mixed = jnp.einsum(
        "whqk,wkhc->wqhc", weights, value_part, preferred_element_type=jnp.float32
    ).astype(jnp.bfloat16)
    return from_windows(mixed.reshape(windows, positions, features), leading, height, breadth)


def block_forward(inputs, gains, qkv_weight, bias_table, rel_index, classes):
    leading, height, breadth, features = inputs.shape
    normed, norm_pull = jax.vjp(lambda data: layer_norm(data, gains), inputs)
    projected = jnp.dot(
        normed.reshape(-1, features), qkv_weight, preferred_element_type=jnp.float32
    ).astype(jnp.bfloat16)
    projected = projected.reshape(leading, height, breadth, 3 * features)
    attended, attend_pull = jax.vjp(
        lambda data: window_attention(data, bias_table, rel_index, classes), projected
    )
    return (attended, norm_pull, attend_pull)


def block_backward(upstream, attended, norm_pull, attend_pull, qkv_weight, out_weight):
    leading, height, breadth, features = upstream.shape
    flat_up = upstream.reshape(-1, features)
    out_term = jnp.dot(
        attended.reshape(-1, features).T, flat_up, preferred_element_type=jnp.float32
    )
    att_grad = jnp.dot(flat_up, out_weight.T, preferred_element_type=jnp.float32).astype(
        jnp.bfloat16
    )
    (proj_grad,) = attend_pull(att_grad.reshape(leading, height, breadth, features))
    normed_grad = jnp.dot(
        proj_grad.reshape(-1, 3 * features), qkv_weight.T, preferred_element_type=jnp.float32
    ).astype(jnp.bfloat16)
    (input_grad,) = norm_pull(normed_grad.reshape(leading, height, breadth, features))
    return (input_grad, out_term)


def gather_weights(qkv_shard, out_shard):
    return (
        lax.all_gather(qkv_shard, ("lat", "lon"), axis=0, tiled=True),
        lax.all_gather(out_shard, ("lat", "lon"), axis=0, tiled=True),
    )


def roll_tile(tensor, direction):
    lat_dim = tensor.ndim - 3
    lon_dim = tensor.ndim - 2
    half = WIN // 2
    height = tensor.shape[lat_dim]
    if direction < 0:
        strip = lax.slice_in_dim(tensor, 0, half, axis=lat_dim)
    else:
        strip = lax.slice_in_dim(tensor, height - half, height, axis=lat_dim)
    arrived = passed_along(strip, "lat", direction)
    if direction < 0:
        tensor = jnp.concatenate(
            [lax.slice_in_dim(tensor, half, height, axis=lat_dim), arrived], axis=lat_dim
        )
    else:
        tensor = jnp.concatenate(
            [arrived, lax.slice_in_dim(tensor, 0, height - half, axis=lat_dim)], axis=lat_dim
        )
    breadth = tensor.shape[lon_dim]
    if direction < 0:
        strip = lax.slice_in_dim(tensor, 0, half, axis=lon_dim)
    else:
        strip = lax.slice_in_dim(tensor, breadth - half, breadth, axis=lon_dim)
    arrived = passed_along(strip, "lon", direction)
    if direction < 0:
        return jnp.concatenate(
            [lax.slice_in_dim(tensor, half, breadth, axis=lon_dim), arrived], axis=lon_dim
        )
    else:
        return jnp.concatenate(
            [arrived, lax.slice_in_dim(tensor, 0, breadth - half, axis=lon_dim)], axis=lon_dim
        )


def reduce_terms(first_term, second_term):
    first_share, second_share = (
        lax.psum_scatter(first_term, ("lat", "lon"), scatter_dimension=0, tiled=True),
        lax.psum_scatter(second_term, ("lat", "lon"), scatter_dimension=0, tiled=True),
    )
    return (
        lax.psum(first_share.astype(jnp.bfloat16), "rep").astype(jnp.float32),
        lax.psum(second_share.astype(jnp.bfloat16), "rep").astype(jnp.float32),
    )


def on_device(
    tokens,
    grad_out,
    first_gain,
    first_qkv_weight,
    first_out_weight,
    first_bias,
    second_gain,
    second_qkv_weight,
    second_out_weight,
    second_bias,
    rel_index,
    classes,
):
    features = tokens.shape[-1]
    first_qkv, first_out = gather_weights(first_qkv_weight, first_out_weight)
    first_att, first_norm_pull, first_att_pull = block_forward(
        tokens, first_gain, first_qkv, first_bias, rel_index, None
    )
    update = jnp.dot(
        first_att.reshape(-1, features), first_out, preferred_element_type=jnp.float32
    ).reshape(tokens.shape)
    middle = (tokens.astype(jnp.float32) + update).astype(jnp.bfloat16)
    second_qkv, second_out = gather_weights(second_qkv_weight, second_out_weight)
    paired = roll_tile(jnp.stack([middle, grad_out]), -1)
    shifted, shifted_grad = (paired[0], paired[1])
    second_att, second_norm_pull, second_att_pull = block_forward(
        shifted, second_gain, second_qkv, second_bias, rel_index, classes
    )
    second_field_grad, second_term = block_backward(
        shifted_grad, second_att, second_norm_pull, second_att_pull, second_qkv, second_out
    )
    returned = roll_tile(second_field_grad, 1)
    middle_grad = (grad_out.astype(jnp.float32) + returned.astype(jnp.float32)).astype(jnp.bfloat16)
    first_field_grad, first_term = block_backward(
        middle_grad, first_att, first_norm_pull, first_att_pull, first_qkv, first_out
    )
    token_grad = (middle_grad.astype(jnp.float32) + first_field_grad.astype(jnp.float32)).astype(
        jnp.bfloat16
    )
    first_total, second_total = reduce_terms(first_term, second_term)
    return (token_grad, first_total, second_total)


def solution(mesh):
    in_specs = (
        P("rep", "lat", "lon", None),
        P("rep", "lat", "lon", None),
        P(),
        P(("lat", "lon"), None),
        P(("lat", "lon"), None),
        P(),
        P(),
        P(("lat", "lon"), None),
        P(("lat", "lon"), None),
        P(),
        P(),
        P("lat", "lon"),
    )
    out_specs = (P("rep", "lat", "lon", None), P(("lat", "lon"), None), P(("lat", "lon"), None))
    return jax.shard_map(
        on_device, mesh=mesh, in_specs=in_specs, out_specs=out_specs, check_vma=False
    )
```

profile of v0, /device:TPU:8, one launch (start us, length us, event | category | flops | bytes accessed | tf_op | source)
XLA Modules:
  0.0 1365.4 jit_solution(15182115810186948251)
XLA Ops:
  15.5 38.7 %gather_fusion = f32[20736,16]{1,0:T(8,128)} fusion(f32[16,529]{0,1:T(8,128)S(1)} %bitcast.156, s32[21504]{0:T(1024)S(1)} %pad_clamp_fusion), kind=kCustom, calls=%fused_computation | custom fusion | bytes 2737152 | tf_op jit(solution)/shard_map/jvp()/gather | solution.py:49
  54.1 11.7 copy.39
  65.8 138.2 %all-gather.5.cloned.1.call-done = bf16[1024,3072]{1,0:T(8,128)(2,1)} async-done(((bf16[16,3072]{1,0:T(8,128)(2,1)}), bf16[1024,3072]{1,0:T(8,128)(2,1)}) %all-gather.5.cloned.1.call-update) | async-done | bytes 6291472 | tf_op jit(solution)/shard_map/all_gather | solution.py:94
  204.0 4.8 convolution_convert_fusion.1
  219.5 172.9 %all-gather.7.cloned.1.call-done = bf16[1024,1024]{1,0:T(8,128)(2,1)} async-done(((bf16[16,1024]{1,0:T(8,128)(2,1)}), bf16[1024,1024]{1,0:T(8,128)(2,1)}) %all-gather.7.cloned.1.call-update) | async-done | bytes 2097168 | tf_op jit(solution)/shard_map/all_gather | solution.py:95
  394.8 5.3 collective-permute-done
  401.2 38.7 %gather_fusion.1 = f32[20736,16]{1,0:T(8,128)} fusion(f32[16,529]{0,1:T(8,128)S(1)} %bitcast.157, s32[21504]{0:T(1024)S(1)} %pad_clamp_fusion), kind=kCustom, calls=%fused_computation.1 | custom fusion | bytes 2737152 | tf_op jit(solution)/shard_map/jvp()/gather | solution.py:49
  439.9 11.7 copy.46
  456.7 131.0 %all-gather.11.cloned.1.call-done = bf16[1024,3072]{1,0:T(8,128)(2,1)} async-done(((bf16[16,3072]{1,0:T(8,128)(2,1)}), bf16[1024,3072]{1,0:T(8,128)(2,1)}) %all-gather.11.cloned.1.call-update) | async-done | bytes 6291472 | tf_op jit(solution)/shard_map/all_gather | solution.py:94
  587.7 5.2 convolution_convert_fusion
  599.4 4.1 convolution_convert_fusion.8
  607.4 173.3 %all-gather.9.cloned.1.call-done = bf16[1024,1024]{1,0:T(8,128)(2,1)} async-done(((bf16[16,1024]{1,0:T(8,128)(2,1)}), bf16[1024,1024]{1,0:T(8,128)(2,1)}) %all-gather.9.cloned.1.call-update) | async-done | bytes 2097168 | tf_op jit(solution)/shard_map/all_gather | solution.py:95
  791.9 4.3 fusion.25
  796.2 4.3 fusion.28
  800.5 4.3 fusion.27
  806.6 5.1 fusion.32
  813.6 9.2 collective-permute-done.2
  823.0 8.5 collective-permute-done.3
  849.2 4.5 fusion.30
  853.8 4.5 fusion.29
  859.9 5.1 fusion.31
  866.0 184.5 %reduce-scatter.5.cloned.1.call-done = f32[16,1024]{1,0:T(8,128)} async-done(((f32[1024,1024]{1,0:T(8,128)}), f32[16,1024]{1,0:T(8,128)}) %reduce-scatter.5.cloned.1.call-update) | async-done | bytes 65552 | tf_op jit(solution)/shard_map/reduce_scatter | solution.py:136
  1052.0 262.1 %reduce-scatter.3.cloned.1.call-done = f32[16,1024]{1,0:T(8,128)} async-done(((f32[1024,1024]{1,0:T(8,128)}), f32[16,1024]{1,0:T(8,128)}) %reduce-scatter.3.cloned.1.call-update) | async-done | bytes 65552 | tf_op jit(solution)/shard_map/reduce_scatter | solution.py:135
  1316.7 39.1 %all-reduce.9.cloned.1.call-done = (bf16[16,1024]{1,0:T(8,128)(2,1)}, bf16[16,1024]{1,0:T(8,128)(2,1)}) async-done(((bf16[16,1024]{1,0:T(8,128)(2,1)}, bf16[16,1024]{1,0:T(8,128)(2,1)}), (bf16[16,1024]{1,0:T(8,128)(2,1)}, bf16[16,1024]{1,0:T(8,128)(2,1)})) %all-reduce.9.cloned.1.call-update) | async-done | bytes 65552 | tf_op jit(solution)/shard_map/psum | solution.py:139
  (160 shorter events, 79.7 us)
Async XLA Ops:
  7.2 7.3 copy-start
  7.2 196.9 %all-gather.5.cloned.1.call-start = ((), (), s32[]{:S(2)}) async-start(), calls=%async_computation.2 | async-start | bytes 6389760 | tf_op jit(solution)/shard_map/all_gather | solution.py:94
  7.9 384.5 %all-gather.7.cloned.1.call-start = ((), (), s32[]{:S(2)}) async-start(), calls=%async_computation.3 | async-start | bytes 2129920 | tf_op jit(solution)/shard_map/all_gather | solution.py:95
  8.7 579.0 %all-gather.11.cloned.1.call-start = ((), (), s32[]{:S(2)}) async-start(), calls=%async_computation.5 | async-start | bytes 6389760 | tf_op jit(solution)/shard_map/all_gather | solution.py:94
  9.4 771.4 %all-gather.9.cloned.1.call-start = ((), (), s32[]{:S(2)}) async-start(), calls=%async_computation.4 | async-start | bytes 2129920 | tf_op jit(solution)/shard_map/all_gather | solution.py:95
  10.0 1040.6 %reduce-scatter.5.cloned.1.call-start = ((), (), s32[]{:S(2)}) async-start(), calls=%async_computation.7 | async-start | bytes 4259840 | tf_op jit(solution)/shard_map/reduce_scatter | solution.py:136
  12.4 41.7 %copy-start.16 = (f32[12,12]{1,0:T(8,128)}, f32[12,12]{1,0:T(8,128)S(1)}, u32[]{:S(2)}) copy-start(f32[12,12]{1,0:T(8,128)S(1)} %fusion.40) | copy-start | bytes 1732
  12.4 41.7 %copy-start.14 = (f32[12,12]{1,0:T(8,128)}, f32[12,12]{1,0:T(8,128)S(1)}, u32[]{:S(2)}) copy-start(f32[12,12]{1,0:T(8,128)S(1)} %fusion.56) | copy-start | bytes 1732
  218.6 176.0 %copy-start.8 = (bf16[16,64,144]{2,1,0:T(8,128)(2,1)}, bf16[16,64,144]{2,1,0:T(8,128)(2,1)S(1)}, u32[]{:S(2)}) copy-start(bf16[16,64,144]{2,1,0:T(8,128)(2,1)S(1)} %convolution_convert_fusion.11) | copy-start | bytes 884740
  219.1 175.5 %copy-start.10 = (bf16[1,12,12,1024]{3,2,1,0:T(8,128)(2,1)S(1)}, bf16[1,12,12,1024]{3,2,1,0:T(8,128)(2,1)}, u32[]{:S(2)}) copy-start(bf16[1,12,12,1024]{3,2,1,0:T(8,128)(2,1)} %param.13) | copy-start | bytes 884740
  394.7 5.4 collective-permute-start
  401.0 51.3 %collective-permute-start.1 = (bf16[2,1,12,6,1024]{4,3,2,1,0:T(8,128)(2,1)}, bf16[2,1,12,6,1024]{4,3,2,1,0:T(8,128)(2,1)}, u32[]{:S(2)}, u32[]{:S(2)}) collective-permute-start(bf16[2,1,12,6,1024]{4,3,2,1,0:T(8,128)(2,1)} %get-tuple-element.8), channel_id=1, source_target_pairs={{4,0},{8,4},{12,8},{16,12},{20,16},{24,20},{28,24},{32,28},{36,32}... | collective-permute-start | bytes 884744 | tf_op jit(solution)/shard_map/ppermute | solution.py:16
  455.4 132.3 %copy-start.26 = (f32[144]{0:T(256)}, f32[144]{0:T(256)S(1)}, u32[]{:S(2)}) copy-start(f32[144]{0:T(256)S(1)} %div.100) | copy-start | bytes 1732
  456.6 131.1 %copy-start.18 = (f32[12,12]{1,0:T(8,128)}, f32[12,12]{1,0:T(8,128)S(1)}, u32[]{:S(2)}) copy-start(f32[12,12]{1,0:T(8,128)S(1)} %multiply_reduce_fusion.1) | copy-start | bytes 1732
  456.7 131.0 %copy-start.30 = (f32[144]{0:T(256)}, f32[144]{0:T(256)S(1)}, u32[]{:S(2)}) copy-start(f32[144]{0:T(256)S(1)} %add.73) | copy-start | bytes 1732
  456.7 131.0 %copy-start.28 = (f32[144]{0:T(256)}, f32[144]{0:T(256)S(1)}, u32[]{:S(2)}) copy-start(f32[144]{0:T(256)S(1)} %rsqrt.27) | copy-start | bytes 1732
  599.4 189.1 %copy-start.24 = (f32[16,144]{1,0:T(8,128)}, f32[16,144]{1,0:T(8,128)S(1)}, u32[]{:S(2)}) copy-start(f32[16,144]{1,0:T(8,128)S(1)} %get-tuple-element.17) | copy-start | bytes 27652
  607.2 706.9 %reduce-scatter.3.cloned.1.call-start = ((), (), s32[]{:S(2)}) async-start(), calls=%async_computation.6 | async-start | bytes 4259840 | tf_op jit(solution)/shard_map/reduce_scatter | solution.py:135
  812.1 19.4 %copy-start.11 = (bf16[1,12,12,1024]{3,2,1,0:T(8,128)(2,1)S(1)}, bf16[1,12,12,1024]{3,2,1,0:T(8,128)(2,1)}, u32[]{:S(2)}) copy-start(bf16[1,12,12,1024]{3,2,1,0:T(8,128)(2,1)} %param.13) | copy-start | bytes 884740
  813.2 18.6 %copy-start.9 = (bf16[16,64,144]{2,1,0:T(8,128)(2,1)S(1)}, bf16[16,64,144]{2,1,0:T(8,128)(2,1)}, u32[]{:S(2)}) copy-start(bf16[16,64,144]{2,1,0:T(8,128)(2,1)} %copy-done.8) | copy-start | bytes 884740
  813.5 9.3 collective-permute-start.2
  822.9 8.6 collective-permute-start.3
  834.5 8.5 copy-start.2
  834.5 521.3 %all-reduce.9.cloned.1.call-start = ((), (), s32[]{:S(2)}) async-start(), calls=%async_computation.8 | async-start | bytes 131072 | tf_op jit(solution)/shard_map/psum | solution.py:139
  (20 other events, 57.0 us)
Sparse Core Ops, SparseCore 0:
  9.8 194.1 all-gather.4
  205.9 186.4 all-gather.6
  394.2 193.4 all-gather.10
  589.4 191.3 all-gather.8
  783.2 267.3 reduce-scatter.4
  1053.1 260.9 reduce-scatter.2
  1317.1 38.6 all-reduce.8
where the time goes:
time: 1370 us
  waiting for transfers between devices  1130 us (82%)
  local copies, waits for them, and re-layouts  121 us (9%)
  matrix products  76.9 us (6%)
  other arithmetic  25.4 us (2%)
  between operations  14.8 us (1%)
    all_gather x2, waiting for transfers between devices, gather_weights(): lax.all_gather(out_shard, ('lat', 'lon'), axis=0, tiled=True)  346 us
    all_gather x2, waiting for transfers between devices, gather_weights(): lax.all_gather(qkv_shard, ('lat', 'lon'), axis=0, tiled=True)  269 us
    reduce_scatter x1, waiting for transfers between devices, reduce_terms(): lax.psum_scatter(first_term, ('lat', 'lon'), scatter_dimension=0, tiled=T...  262 us
    reduce_scatter x1, waiting for transfers between devices, reduce_terms(): lax.psum_scatter(second_term, ('lat', 'lon'), scatter_dimension=0, tiled=...  185 us
    gather x4, local copies, waits for them, and re-layouts, window_attention(): scores = scores + jnp.transpose(bias_table)[:, rel_index][None]  101 us
    psum x1, waiting for transfers between devices, reduce_terms(): lax.psum(first_share.astype(jnp.bfloat16), 'rep').astype(jnp.float32)  39.1 us
  transfers between devices with their start and end apart: 11, of which 10 were waited for; matrix products, arithmetic and copies ran while one was open for 16% of the time, Pallas kernels for 0%

commit v1 on v0

v1 whole, which is shorter than its diff:
```python
import jax
import jax.numpy as jnp
from jax import lax
from jax.experimental import pallas as pl
from jax.experimental.pallas import tpu as pltpu
from jax.sharding import PartitionSpec as P

HEADS = 16
WIN = 12
HALF = WIN // 2
TOK = WIN * WIN
QUARTER = HALF * HALF
D = 1024
EPSILON = 1e-05
NX, NY, NZ = 4, 4, 8
TABLE = 640
BLOCK = 256
LOW = -1e30
MESH = pl.DeviceIdType.MESH
F32 = jnp.float32
BF16 = jnp.bfloat16

ORDERS = ("zx", "xz", "zx", "xz", "zx", "xz", "zx", "zx")
STARTS = (0, 0, 0, 1, 3, 3, 3, 4)
STAGES = 8


def dot(a, b):
    return jnp.dot(a, b, preferred_element_type=F32)


def dot_t(a, b):
    return lax.dot_general(a, b, (((1,), (1,)), ((), ())), preferred_element_type=F32)


def t_dot(a, b):
    return lax.dot_general(a, b, (((0,), (0,)), ((), ())), preferred_element_type=F32)


def iota(shape, dim):
    return lax.broadcasted_iota(jnp.int32, shape, dim)


def over_six(n):
    return (n * 10923) >> 16


def norm_parts(x):
    centered = x - jnp.mean(x, axis=-1, keepdims=True)
    scale = lax.rsqrt(jnp.mean(centered * centered, axis=-1, keepdims=True) + EPSILON)
    return centered * scale, scale


def norm_back(x, gain, grad):
    unit, scale = norm_parts(x)
    g = grad * gain
    return scale * (
        g - jnp.mean(g, axis=-1, keepdims=True) - unit * jnp.mean(g * unit, axis=-1, keepdims=True)
    )


def kernel(
    tokens_ref, grad_ref, gain1_ref, gain2_ref, wq1_ref, wo1_ref, wq2_ref, wo2_ref,
    tab_ref, rel_ref, cls_ref,
    out_ref, og1_ref, og2_ref,
    wbuf, bias, idx_u, u_raw, u_ref, same, probs, qkv, dqkv, norm_buf, datt,
    tok_f, go_f, mid_f, sh_f, tmp_f, g_stack, att_stack, roll_s, roll_r,
    xs, xr, zs, zr, ys,
    w_local, w_send, w_recv, roll_send, roll_recv, sib_send, sib_recv,
    x_send, x_recv, z_send, z_recv, y_send, y_recv,
):
    lat, lon, y = lax.axis_index("lat"), lax.axis_index("lon"), lax.axis_index("rep")
    xh, core = lat // 2, lat % 2
    z, xl = lon // 2, lon % 2
    x = xh * 2 + xl
    other = 1 - core

    def at_x(d):
        n = (x + d) % NX
        return ((n // 2) * 2 + core, z * 2 + n % 2, y)

    def at_z(d):
        return (lat, ((z + d) % NZ) * 2 + xl, y)

    def at_y(d):
        return (lat, lon, (y + d) % NY)

    sibling = (xh * 2 + other, lon, y)

    def at_roll(a, b):
        return ((lat + a + 4) % 4, (lon + b + 16) % 16, y)

    def copy(src, dst, send, recv, device):
        return pltpu.make_async_remote_copy(
            src_ref=src, dst_ref=dst, send_sem=send, recv_sem=recv,
            device_id=device, device_id_type=MESH,
        )

    local = []
    for u in range(8):
        source = (wq1_ref, wo1_ref, wq2_ref, wo2_ref)[(u // 4) * 2 + (u % 4) // 3]
        column = (u % 4) * D if u % 4 < 3 else 0
        local.append(
            pltpu.make_async_copy(
                source.at[:, pl.ds(column, D)], wbuf.at[u, xh, core, z, xl], w_local.at[u]
            )
        )
        local[-1].start()

    barrier = pltpu.get_barrier_semaphore()
    partners = [at_z(d) for d in range(1, NZ)] + [at_x(d) for d in range(1, NX)]
    partners += [at_y(d) for d in range(1, NY)] + [sibling]
    partners += [at_roll(*s) for s in ((1, 0), (-1, 0), (0, 1), (0, -1), (1, 1), (-1, -1))]
    for partner in partners:
        pl.semaphore_signal(barrier, inc=1, device_id=partner, device_id_type=MESH)
    pl.semaphore_wait(barrier, len(partners))
    for c in local:
        c.wait()

    flights = {}

    def send(u, k, name, src, dst_device):
        c = copy(src, src, w_send.at[u, k], w_recv.at[u, k], dst_device)
        c.start()
        flights[u, name] = c

    def got(u, name):
        flights[u, name].wait_recv()

    def element(u, nx, nz):
        nx = (nx + NX) % NX
        return wbuf.at[u, nx // 2, core, (nz + NZ) % NZ, nx % 2]

    def column(u, nx, first, count):
        nx = (nx + NX) % NX
        return wbuf.at[u, nx // 2, core, pl.ds(first, count), nx % 2]

    def part(u, nx, first):
        nx = (nx + NX) % NX
        return wbuf.at[u, nx // 2, core, z, nx % 2, :, pl.ds(first, 512)]

    def group(u, nz):
        return wbuf.at[u, :, core, (nz + NZ) % NZ]

    def ring_z(u, piece, stage):
        far_right = u % 2 == 0
        if stage > 0:
            if stage < 4 or far_right:
                got(u, f"r{stage}")
            if stage < 4 or not far_right:
                got(u, f"l{stage}")
        if stage < 3 or (stage == 3 and far_right):
            send(u, stage, f"r{stage + 1}", piece(u, z - stage), at_z(1))
        if stage < 3 or (stage == 3 and not far_right):
            send(u, 4 + stage if stage < 3 else 3, f"l{stage + 1}", piece(u, z + stage), at_z(-1 + NZ))

    def share(u):
        send(u, 11, "s", wbuf.at[u, :, core], sibling)

    def gather_stage(u, stage):
        if stage < 0 or stage >= STAGES:
            return
        if ORDERS[u] == "zx":
            if stage <= 4:
                ring_z(u, lambda u, n: element(u, x, n), stage)
            if stage == 4:
                send(u, 7, "xr1", column(u, x, 0, NZ), at_x(1))
                send(u, 8, "xl1", column(u, x, 0, NZ), at_x(3))
            if stage == 5:
                got(u, "xr1")
                send(u, 9, "xr2", column(u, x - 1, 0, 4), at_x(1))
                got(u, "xl1")
                send(u, 10, "xl2", column(u, x + 1, 4, 4), at_x(3))
            if stage == 6:
                got(u, "xr2")
                got(u, "xl2")
                share(u)
        else:
            if stage == 0:
                send(u, 7, "xr1", element(u, x, z), at_x(1))
                send(u, 8, "xl1", element(u, x, z), at_x(3))
            if stage == 1:
                got(u, "xr1")
                send(u, 9, "xr2", part(u, x - 1, 0), at_x(1))
                got(u, "xl1")
                send(u, 10, "xl2", part(u, x + 1, 512), at_x(3))
            if stage == 2:
                got(u, "xr2")
                got(u, "xl2")
            if 2 <= stage <= 6:
                ring_z(u, group, stage - 2)
            if stage == 6:
                share(u)
        if stage == 7:
            got(u, "s")

    clock = [0]

    def gather_turn():
        for u in range(8):
            gather_stage(u, clock[0] - STARTS[u])
        clock[0] += 1

    def gather_until(units):
        while clock[0] < max(STARTS[u] for u in units) + STAGES:
            gather_turn()

    gather_turn()

    for r in range(WIN):
        for source, target in ((tokens_ref, tok_f), (grad_ref, go_f)):
            rows = source[0, r].astype(F32)
            target[pl.ds(r * HALF, HALF), :] = rows[:HALF]
            target[pl.ds(72 + r * HALF, HALF), :] = rows[HALF:]

    rolls = {}

    def roll_out(which, source, back):
        to = 1 if back else -1
        places = ((1, (to, 0)), (2, (0, to)), (3, (to, to))) if back else (
            (2, (to, 0)), (1, (0, to)), (0, (to, to)))
        for i, (quarter, shift) in enumerate(places):
            roll_s[which, i, pl.ds(0, QUARTER), :] = source[
                pl.ds(quarter * QUARTER, QUARTER), :].astype(BF16)
            c = copy(roll_s.at[which, i], roll_r.at[which, i],
                     roll_send.at[which, i], roll_recv.at[which, i], at_roll(*shift))
            c.start()
            rolls[which, i] = c

    def roll_in(which, i):
        rolls[which, i].wait_recv()
        return roll_r[which, i, pl.ds(0, QUARTER), :].astype(F32)

    for which in range(3):
        for i in range(3):
            roll_s[which, i, pl.ds(32, 16), :] = jnp.zeros((16, D), BF16)
    roll_out(0, go_f, False)
    gather_turn()

    k_of = iota((TOK, 512), 0)
    lane = iota((TOK, 512), 1)
    side = (lane >= 256).astype(jnp.int32)
    j = lane - side * (256 + 72)
    s = over_six(jnp.maximum(j, 0))
    c = side * HALF + j - s * HALF
    inside = (j >= 0) & (j < 138)
    late = s > 11
    wanted = jnp.where(late, s - 11, s) * WIN + c
    hit = inside & (k_of == wanted)
    pick_a = jnp.where(hit & (s <= 11), 1.0, 0.0).astype(BF16)
    pick_b = jnp.where(hit & late, 1.0, 0.0).astype(BF16)
    high_a = dot((rel_ref[pl.ds(TOK - WIN, WIN), :] >> 4).astype(F32).astype(BF16), pick_a)
    low_a = dot((rel_ref[pl.ds(TOK - WIN, WIN), :] & 15).astype(F32).astype(BF16), pick_a)
    high_b = dot((rel_ref[pl.ds(0, WIN), :] >> 4).astype(F32).astype(BF16), pick_b)
    low_b = dot((rel_ref[pl.ds(0, WIN), :] & 15).astype(F32).astype(BF16), pick_b)
    idx_u[pl.ds(0, WIN), :] = ((high_a + high_b) * 16.0 + low_a + low_b).astype(jnp.int32)
    gather_turn()

    table = tab_ref[...]
    t_high = table.astype(BF16)
    rest = table - t_high.astype(F32)
    t_mid = rest.astype(BF16)
    t_low = (rest - t_mid.astype(F32)).astype(BF16)
    parts = jnp.concatenate([t_high, t_mid, t_low], axis=0)

    def choose(c1, _):
        chosen = idx_u[pl.ds(c1, 1), :]
        onehot = jnp.where(iota((TABLE, 512), 0) == chosen, 1.0, 0.0).astype(BF16)
        got3 = dot(parts, onehot)
        u_raw[c1] = got3[0:32] + got3[32:64] + got3[64:96]
        return 0

    lax.fori_loop(0, WIN, choose, 0)
    gather_turn()
    for th in range(2 * HEADS):
        rows = u_raw[:, th, :]
        u_ref[th, pl.ds(0, HALF), :] = rows[:HALF]
        u_ref[th, pl.ds(8, HALF), :] = rows[HALF:]

    def slide(th, _):
        left, right = u_ref[th, :, pl.ds(0, 256)], u_ref[th, :, pl.ds(256, 256)]
        first = iota((16, 256), 1) < 72
        for r in range(WIN):
            shift = (256 - HALF * (11 - r)) % 256
            a = pltpu.roll(left, shift, 1) if shift else left
            b = pltpu.roll(right, shift, 1) if shift else right
            value = jnp.where(first, a, b)[:, :TOK]
            bias[th, pl.ds(r * HALF, HALF), :] = value[:HALF]
            bias[th, pl.ds(72 + r * HALF, HALF), :] = value[8:8 + HALF]
        return 0

    lax.fori_loop(0, HEADS, slide, 0)
    gather_turn()

    n = iota((TOK, WIN), 0)
    right_half = (n >= 72).astype(jnp.int32)
    n = n - 72 * right_half
    row_of = over_six(n)
    col_of = right_half * HALF + n - row_of * HALF
    row_pick = jnp.where(iota((TOK, WIN), 1) == row_of, 1.0, 0.0).astype(BF16)
    per_row = dot(row_pick, cls_ref[...].astype(F32).astype(BF16))
    label = jnp.sum(
        jnp.where(iota((TOK, WIN), 1) == col_of, per_row, 0.0), axis=1, keepdims=True)
    member = jnp.where(iota((TOK, 128), 1) == label.astype(jnp.int32), 1.0, 0.0).astype(BF16)
    same[...] = dot_t(member, member)

    lax.fori_loop(HEADS, 2 * HEADS, slide, 0)

    even = jnp.where(iota((1, 128), 1) < 64, 1.0, 0.0).astype(BF16)
    masks = (even, (1.0 - even.astype(F32)).astype(BF16))

    def weight(u, first):
        return wbuf[u, :, :, :, :, :, pl.ds(first, BLOCK)].reshape(D, BLOCK)

    def weight_rows(u, block):
        return wbuf[u, block // 2, block % 2].reshape(BLOCK, D)

    def project(which):
        for u in range(3):
            def step(i, _):
                first = pl.multiple_of(i * BLOCK, BLOCK)
                result = dot(norm_buf[...], weight(which * 4 + u, first))
                qkv[which, :, pl.ds(pl.multiple_of(u * D + first, BLOCK), BLOCK)] = result.astype(BF16)
                return 0
            lax.fori_loop(0, D // BLOCK, step, 0)

    def lanes(i, offset=0):
        return pl.ds(pl.multiple_of(offset + i * 128, 128), 128)

    def attend(which):
        def step(i, _):
            q2 = qkv[which, :, lanes(i)]
            k2 = qkv[which, :, lanes(i, D)]
            v2 = qkv[which, :, lanes(i, 2 * D)]
            mixed = None
            for e in range(2):
                score = dot_t(q2 * masks[e], k2) * 0.125 + bias[which * HEADS + 2 * i + e]
                if which:
                    score = jnp.where(same[...] > 0.5, score, LOW)
                power = jnp.exp(score - jnp.max(score, axis=1, keepdims=True))
                share_of = (power * (1.0 / jnp.sum(power, axis=1, keepdims=True))).astype(BF16)
                probs[which * HEADS + 2 * i + e] = share_of
                term = dot(share_of, v2 * masks[e])
                mixed = term if mixed is None else mixed + term
            att_stack[which, i // 2, pl.ds(0, TOK), lanes(i % 2)] = mixed.astype(BF16)
            return 0
        lax.fori_loop(0, HEADS // 2, step, 0)

    def attend_back(which):
        def step(i, _):
            q2 = qkv[which, :, lanes(i)]
            k2 = qkv[which, :, lanes(i, D)]
            v2 = qkv[which, :, lanes(i, 2 * D)]
            do2 = datt[:, lanes(i)]
            dq = dk = dv = None
            for e in range(2):
                share_of = probs[which * HEADS + 2 * i + e]
                up = do2 * masks[e]
                dp = dot_t(up, v2)
                share_f = share_of.astype(F32)
                mean = jnp.sum(dp * share_f, axis=1, keepdims=True)
                ds = (share_f * (dp - mean) * 0.125).astype(BF16)
                a = t_dot(share_of, up)
                b = dot(ds, k2 * masks[e])
                c = t_dot(ds, q2 * masks[e])
                dv = a if dv is None else dv + a
                dq = b if dq is None else dq + b
                dk = c if dk is None else dk + c
            dqkv[:, lanes(i)] = dq.astype(BF16)
            dqkv[:, lanes(i, D)] = dk.astype(BF16)
            dqkv[:, lanes(i, 2 * D)] = dv.astype(BF16)
            return 0
        lax.fori_loop(0, HEADS // 2, step, 0)

    def att_grad(which):
        for b in range(4):
            datt[:, pl.ds(b * BLOCK, BLOCK)] = dot_t(
                g_stack[which, pl.ds(0, TOK), :], weight_rows(which * 4 + 3, b)).astype(BF16)

    def normed_grad(which):
        for b in range(4):
            result = None
            for u in range(3):
                term = dot_t(dqkv[:, pl.ds(u * D, D)], weight_rows(which * 4 + u, b))
                result = term if result is None else result + term
            tmp_f[:, pl.ds(b * BLOCK, BLOCK)] = result.astype(BF16).astype(F32)

    sibs = {}

    def to_sibling(name, k, src, dst):
        c = copy(src, dst, sib_send.at[k], sib_recv.at[k], sibling)
        c.start()
        sibs[name] = c

    def send_att(m):
        for h in range(2):
            to_sibling((m, h), m * 3 + h, att_stack.at[m, h * 2 + other, pl.ds(0, TOK)],
                       att_stack.at[m, h * 2 + other, pl.ds(TOK, TOK)])

    def send_grad(m):
        to_sibling((m, 2), m * 3 + 2, g_stack.at[m, pl.ds(0, TOK)], g_stack.at[m, pl.ds(TOK, TOK)])

    xflights, zflights, yflights = {}, {}, {}

    def reduce_x(m):
        for k in range(3):
            sibs[m, k].wait_recv()
        for h in range(2):
            def step(i, _):
                cols = pl.ds(pl.multiple_of(i * BLOCK, BLOCK), BLOCK)
                result = t_dot(att_stack[m, h * 2 + core], g_stack[m, :, cols]).astype(BF16)
                xs[m, h, :, :, :, cols] = result.reshape(NZ, 2, 16, BLOCK)
                return 0
            lax.fori_loop(0, D // BLOCK, step, 0)
        for d in (2, 1, 3):
            target = (x + d) % NX
            c = copy(xs.at[m, target // 2, :, target % 2], xr.at[m, d - 1],
                     x_send.at[m, d - 1], x_recv.at[m, d - 1], at_x(d))
            c.start()
            xflights[m, d] = c

    def reduce_z(m):
        for d in range(1, NX):
            xflights[m, d].wait_recv()

        def step(i, _):
            value = xs[m, xh, i, xl].astype(F32)
            for d in range(NX - 1):
                value = value + xr[m, d, i].astype(F32)
            zs[m, i] = value.astype(BF16)
            return 0
        lax.fori_loop(0, NZ, step, 0)
        for d in (4, 3, 5, 2, 6, 1, 7):
            c = copy(zs.at[m, (z + d) % NZ], zr.at[m, d - 1],
                     z_send.at[m, d - 1], z_recv.at[m, d - 1], at_z(d))
            c.start()
            zflights[m, d] = c

    def reduce_y(m):
        for d in range(1, NZ):
            zflights[m, d].wait_recv()
        value = zs[m, z].astype(F32)
        for d in range(NZ - 1):
            value = value + zr[m, d].astype(F32)
        ys[m, y] = value.astype(BF16)
        for d in range(1, NY):
            c = copy(ys.at[m, y], ys.at[m, y], y_send.at[m, d - 1], y_recv.at[m, d - 1], at_y(d))
            c.start()
            yflights[m, d] = c

    def reduce_end(m, target):
        for d in range(1, NY):
            yflights[m, d].wait_recv()
        value = ys[m, 0].astype(F32)
        for i in range(1, NY):
            value = value + ys[m, i].astype(F32)
        target[...] = value

    unit, _ = norm_parts(tok_f[...])
    norm_buf[...] = (unit * gain1_ref[...]).astype(BF16)
    gather_until((0, 1, 2))
    project(0)
    gather_turn()
    attend(0)
    send_att(0)
    gather_until((3,))
    for b in range(4):
        cols = pl.ds(b * BLOCK, BLOCK)
        result = tok_f[:, cols]
        for h in range(4):
            result = result + dot(att_stack[0, h, pl.ds(0, TOK), :],
                                  wbuf[3, h // 2, h % 2, :, :, :, cols].reshape(BLOCK, BLOCK))
        mid_f[:, cols] = result.astype(BF16).astype(F32)
    roll_out(1, mid_f, False)
    sh_f[pl.ds(0, QUARTER), :] = go_f[pl.ds(3 * QUARTER, QUARTER), :]
    for i in range(3):
        sh_f[pl.ds((i + 1) * QUARTER, QUARTER), :] = roll_in(0, i)
    g_stack[1, pl.ds(0, TOK), :] = sh_f[...].astype(BF16)
    send_grad(1)
    gather_until(range(8))
    att_grad(1)
    sh_f[pl.ds(0, QUARTER), :] = mid_f[pl.ds(3 * QUARTER, QUARTER), :]
    for i in range(3):
        sh_f[pl.ds((i + 1) * QUARTER, QUARTER), :] = roll_in(1, i)
    unit, _ = norm_parts(sh_f[...])
    norm_buf[...] = (unit * gain2_ref[...]).astype(BF16)
    project(1)
    attend(1)
    send_att(1)
    attend_back(1)
    reduce_x(1)
    normed_grad(1)
    mid_f[...] = norm_back(sh_f[...], gain2_ref[...], tmp_f[...])
    roll_out(2, mid_f, True)
    sh_f[pl.ds(3 * QUARTER, QUARTER), :] = mid_f[pl.ds(0, QUARTER), :].astype(BF16).astype(F32)
    reduce_z(1)
    for i, quarter in enumerate((2, 1, 0)):
        sh_f[pl.ds(quarter * QUARTER, QUARTER), :] = roll_in(2, i)
    mid_f[...] = (go_f[...] + sh_f[...]).astype(BF16).astype(F32)
    g_stack[0, pl.ds(0, TOK), :] = mid_f[...].astype(BF16)
    send_grad(0)
    att_grad(0)
    reduce_x(0)
    attend_back(0)
    reduce_y(1)
    normed_grad(0)
    reduce_z(0)
    sh_f[...] = mid_f[...] + norm_back(tok_f[...], gain1_ref[...], tmp_f[...]).astype(BF16).astype(F32)
    for r in range(WIN):
        rows = jnp.concatenate(
            [sh_f[pl.ds(r * HALF, HALF), :], sh_f[pl.ds(72 + r * HALF, HALF), :]], axis=0)
        out_ref[0, r] = rows.astype(BF16)
    reduce_end(1, og2_ref)
    reduce_y(0)
    reduce_end(0, og1_ref)
    for group_of in (flights, rolls, sibs, xflights, zflights, yflights):
        for c in group_of.values():
            c.wait_send()


def on_device(
    tokens, grad_out, first_gain, first_qkv_weight, first_out_weight, first_bias,
    second_gain, second_qkv_weight, second_out_weight, second_bias, rel_index, classes,
):
    table = jnp.concatenate([first_bias, second_bias], axis=1).T
    table = jnp.pad(table, ((0, 0), (0, TABLE - table.shape[1])))
    vmem = pl.BlockSpec(memory_space=pltpu.VMEM)
    hbm = pl.BlockSpec(memory_space=pl.ANY)
    dma = pltpu.SemaphoreType.DMA
    return pl.pallas_call(
        kernel,
        out_shape=(
            jax.ShapeDtypeStruct((1, WIN, WIN, D), BF16),
            jax.ShapeDtypeStruct((16, D), F32),
            jax.ShapeDtypeStruct((16, D), F32),
        ),
        in_specs=[vmem] * 4 + [hbm] * 4 + [vmem] * 3,
        out_specs=(vmem, vmem, vmem),
        scratch_shapes=[
            pltpu.VMEM((8, 2, 2, NZ, 2, 16, D), BF16),
            pltpu.VMEM((2 * HEADS, TOK, TOK), F32),
            pltpu.VMEM((16, 512), jnp.int32),
            pltpu.VMEM((WIN, 2 * HEADS, 512), F32),
            pltpu.VMEM((2 * HEADS, 16, 512), F32),
            pltpu.VMEM((TOK, TOK), F32),
            pltpu.VMEM((2 * HEADS, TOK, TOK), BF16),
            pltpu.VMEM((2, TOK, 3 * D), BF16),
            pltpu.VMEM((TOK, 3 * D), BF16),
            pltpu.VMEM((TOK, D), BF16),
            pltpu.VMEM((TOK, D), BF16),
            pltpu.VMEM((TOK, D), F32),
            pltpu.VMEM((TOK, D), F32),
            pltpu.VMEM((TOK, D), F32),
            pltpu.VMEM((TOK, D), F32),
            pltpu.VMEM((TOK, D), F32),
            pltpu.VMEM((2, 2 * TOK, D), BF16),
            pltpu.VMEM((2, 4, 2 * TOK, BLOCK), BF16),
            pltpu.VMEM((3, 3, 48, D), BF16),
            pltpu.VMEM((3, 3, 48, D), BF16),
            pltpu.VMEM((2, 2, NZ, 2, 16, D), BF16),
            pltpu.VMEM((2, NX - 1, NZ, 16, D), BF16),
            pltpu.VMEM((2, NZ, 16, D), BF16),
            pltpu.VMEM((2, NZ - 1, 16, D), BF16),
            pltpu.VMEM((2, NY, 16, D), BF16),
            dma((8,)),
            dma((8, 12)), dma((8, 12)),
            dma((3, 3)), dma((3, 3)),
            dma((6,)), dma((6,)),
            dma((2, NX - 1)), dma((2, NX - 1)),
            dma((2, NZ - 1)), dma((2, NZ - 1)),
            dma((2, NY - 1)), dma((2, NY - 1)),
        ],
        compiler_params=pltpu.CompilerParams(
            collective_id=0, has_side_effects=True, vmem_limit_bytes=56 * 1024 * 1024
        ),
        name="window_blocks",
    )(
        tokens, grad_out, first_gain[None], second_gain[None],
        first_qkv_weight, first_out_weight, second_qkv_weight, second_out_weight,
        table, rel_index, classes,
    )


def solution(mesh):
    tile = P("rep", "lat", "lon", None)
    rows = P(("lat", "lon"), None)
    in_specs = (tile, tile, P(), rows, rows, P(), P(), rows, rows, P(), P(), P("lat", "lon"))
    return jax.shard_map(
        on_device, mesh=mesh, in_specs=in_specs, out_specs=(tile, rows, rows), check_vma=False
    )
```

time: 1370 us -> 157 us (0.11)
  waiting for transfers between devices: 1130 us -> 0 us
  Pallas kernels: 0 us -> 150 us
  local copies, waits for them, and re-layouts: 121 us -> 3.93 us
  matrix products: 76.9 us -> 0 us
  other arithmetic: 25.4 us -> 0.81 us
  between operations: 14.8 us -> 0.65 us
    all_gather x4 -> x0, waiting for transfers between devices: 615 us -> none  [the longest x2 346 us: gather_weights(): lax.all_gather(out_shard, ('lat', 'lon'), axis=0, tiled=True)]
    reduce_scatter x2 -> x0, waiting for transfers between devices: 447 us -> none  [the longest x1 262 us: reduce_terms(): lax.psum_scatter(first_term, ('lat', 'lon'), scatter_dimension=0, tiled=T...]
    pallas_call x0 -> x1, Pallas kernels: none -> 150 us  [on_device(): pl.pallas_call(kernel, out_shape=(jax.ShapeDtypeStruct((1, WIN, WIN, D),...]
    gather x4 -> x0, local copies, waits for them, and re-layouts: 101 us -> none  [window_attention(): scores = scores + jnp.transpose(bias_table)[:, rel_index][None]]
    dot_general x21 -> x0, matrix products: 76.9 us -> none  [the longest x6 21.2 us: window_attention(): jnp.einsum('wqhc,wkhc->whqk', query_part, key_part, preferred_element_typ...]
    psum x1 -> x0, waiting for transfers between devices: 39.1 us -> none  [reduce_terms(): lax.psum(first_share.astype(jnp.bfloat16), 'rep').astype(jnp.float32)]
    ppermute x4 -> x0, waiting for transfers between devices: 23 us -> none  [passed_along(): return lax.ppermute(block, axis, route)]
    another operation x8 -> x0, local copies, waits for them, and re-layouts: 15.2 us -> none
  transfers between devices with their start and end apart: 11 -> 0, of which waited for: 10 -> 0; matrix products, arithmetic and copies ran while one was open for 16% -> 0% of each run, Pallas kernels for 0% -> 0%
where the time goes in v1:
time: 157 us; the launch traced here: 156 us
  Pallas kernels  150 us (96%)
  local copies, waits for them, and re-layouts  3.93 us (3%)
    pallas_call x1, Pallas kernels, on_device(): pl.pallas_call(kernel, out_shape=(jax.ShapeDtypeStruct((1, WIN, WIN, D),...  150 us
    unnamed x7, local copies, waits for them, and re-layouts  3.29 us

profile of v1, /device:TPU:8, one launch (start us, length us, event | category | flops | bytes accessed | tf_op | source)
XLA Modules:
  0.0 155.8 jit_solution(12912813079361398616)
XLA Ops:
  0.6 0.8 maximum_bitcast_fusion
  1.4 0.6 pad.4.tab_ref
  2.1 150.4 %window_blocks.1 = (bf16[1,12,12,1024]{3,2,1,0:T(8,128)(2,1)}, f32[16,1024]{1,0:T(8,128)}, f32[16,1024]{1,0:T(8,128)}) custom-call(bf16[1,12,12,1024]{3,2,1,0:T(8,128)(2,1)} %tokens_ref.1, bf16[1,12,12,1024]{3,2,1,0:T(8,128)(2,1)} %grad_ref.1, f32[1,1024]{1,0:T(1,128)} %bitcast.4, f32[1,1024]{1,0:T(1,128)} %bitcast.5, bf16[16,3072]{1,0:T(8,128)(2,1)} %wq1_ref.1, ...), custom_call_target="tpu_custom_call" | custom-call | tf_op jit(solution)/shard_map/window_blocks/pallas_call | solution.py:530
  152.5 0.0 copy-start.1
  152.5 1.8 %copy.18 = bf16[1,12,12,1024]{3,2,1,0:T(8,128)(2,1)} copy(bf16[1,12,12,1024]{3,2,1,0:T(8,128)(2,1)} %get-tuple-element.6) | data formatting | bytes 589824
  154.3 0.0 copy-done.1
  154.3 0.0 copy-start
  154.3 0.6 copy.19
  154.9 0.2 copy-done
  155.1 0.6 copy.20
Async XLA Ops:
  152.5 1.8 %copy-start.1 = (f32[16,1024]{1,0:T(8,128)S(1)}, f32[16,1024]{1,0:T(8,128)}, u32[]{:S(2)}) copy-start(f32[16,1024]{1,0:T(8,128)} %get-tuple-element.7) | copy-start | bytes 196612
  154.3 0.9 copy-start

commit v2 on v1

--- a/solution.py
+++ b/solution.py
@@ -20,9 +20,9 @@
 F32 = jnp.float32
 BF16 = jnp.bfloat16
 
-ORDERS = ("zx", "xz", "zx", "xz", "zx", "xz", "zx", "zx")
-STARTS = (0, 0, 0, 1, 3, 3, 3, 4)
-STAGES = 8
+ORDERS = ("zxy", "zyx", "xyz", "zxy", "zyx", "zxy", "xyz", "zyx")
+STARTS = (0, 0, 0, 1, 1, 2, 2, 2)
+STAGES = 6
 
 
 def dot(a, b):
@@ -65,9 +65,8 @@
     out_ref, og1_ref, og2_ref,
     wbuf, bias, idx_u, u_raw, u_ref, same, probs, qkv, dqkv, norm_buf, datt,
     tok_f, go_f, mid_f, sh_f, tmp_f, g_stack, att_stack, roll_s, roll_r,
-    xs, xr, zs, zr, ys,
-    w_local, w_send, w_recv, roll_send, roll_recv, sib_send, sib_recv,
-    x_send, x_recv, z_send, z_recv, y_send, y_recv,
+    att_t, early, xs, xr, zs, zr, ys, vs, vr, ws, wr, us, ur, os,
+    w_local, w_send, w_recv, roll_send, roll_recv, sib_send, sib_recv, red_send, red_recv,
 ):
     lat, lon, y = lax.axis_index("lat"), lax.axis_index("lon"), lax.axis_index("rep")
     xh, core = lat // 2, lat % 2
@@ -102,7 +101,8 @@
         column = (u % 4) * D if u % 4 < 3 else 0
         local.append(
             pltpu.make_async_copy(
-                source.at[:, pl.ds(column, D)], wbuf.at[u, xh, core, z, xl], w_local.at[u]
+                source.at[:, pl.ds(pl.multiple_of(column + y * BLOCK, BLOCK), BLOCK)],
+                wbuf.at[u, y, xh, core, z, xl], w_local.at[u],
             )
         )
         local[-1].start()
@@ -117,82 +117,141 @@
     for c in local:
         c.wait()
 
-    flights = {}
-
-    def send(u, k, name, src, dst_device):
-        c = copy(src, src, w_send.at[u, k], w_recv.at[u, k], dst_device)
+    flights, counts = {}, [0] * 8
+
+    def send(u, tag, src, device):
+        k = counts[u]
+        counts[u] += 1
+        c = copy(src, src, w_send.at[u, k], w_recv.at[u, k], device)
         c.start()
-        flights[u, name] = c
-
-    def got(u, name):
-        flights[u, name].wait_recv()
-
-    def element(u, nx, nz):
-        nx = (nx + NX) % NX
-        return wbuf.at[u, nx // 2, core, (nz + NZ) % NZ, nx % 2]
-
-    def column(u, nx, first, count):
-        nx = (nx + NX) % NX
-        return wbuf.at[u, nx // 2, core, pl.ds(first, count), nx % 2]
-
-    def part(u, nx, first):
-        nx = (nx + NX) % NX
-        return wbuf.at[u, nx // 2, core, z, nx % 2, :, pl.ds(first, 512)]
-
-    def group(u, nz):
-        return wbuf.at[u, :, core, (nz + NZ) % NZ]
-
-    def ring_z(u, piece, stage):
-        far_right = u % 2 == 0
-        if stage > 0:
-            if stage < 4 or far_right:
-                got(u, f"r{stage}")
-            if stage < 4 or not far_right:
-                got(u, f"l{stage}")
-        if stage < 3 or (stage == 3 and far_right):
-            send(u, stage, f"r{stage + 1}", piece(u, z - stage), at_z(1))
-        if stage < 3 or (stage == 3 and not far_right):
-            send(u, 4 + stage if stage < 3 else 3, f"l{stage + 1}", piece(u, z + stage), at_z(-1 + NZ))
-
-    def share(u):
-        send(u, 11, "s", wbuf.at[u, :, core], sibling)
+        flights[u, k] = c
+        waits.setdefault((u, tag), []).append(c)
+
+    waits = {}
+
+    def got(u, tag):
+        for c in waits[u, tag]:
+            c.wait_recv()
+
+    def element(u):
+        return wbuf.at[u, y, xh, core, z, xl]
+
+    def wrap(n, size):
+        return (n + size) % size
+
+    def spread(u, tag, src, at, size):
+        for d in sorted(range(1, size), key=lambda d: -min(d, size - d)):
+            send(u, tag, src, at(d))
+
+    def share(u, src):
+        send(u, "share", src, sibling)
+
+    def stage_zxy(u, stage):
+        def plane(d):
+            return wbuf.at[u, wrap(y + d, NY), :, core]
+
+        def half(d, h):
+            return wbuf.at[u, wrap(y + d, NY), h, core]
+
+        if stage == 0:
+            spread(u, 0, element(u), at_z, NZ)
+        if stage == 1:
+            got(u, 0)
+            spread(u, 1, wbuf.at[u, y, xh, core, :, xl], at_x, NX)
+        if stage == 2:
+            got(u, 1)
+            send(u, "r1", half(0, 0), at_y(1))
+            send(u, "l1", half(0, 1), at_y(3))
+            send(u, "r2", half(0, 1), at_y(1))
+            send(u, "l2", half(0, 0), at_y(3))
+            share(u, plane(0))
+        if stage == 3:
+            got(u, "r1")
+            send(u, "far", half(-1, 0), at_y(1))
+            got(u, "l1")
+            send(u, "far", half(1, 1), at_y(3))
+            got(u, "r2")
+            share(u, plane(-1))
+            got(u, "l2")
+            share(u, plane(1))
+        if stage == 4:
+            got(u, "far")
+            share(u, plane(2))
+
+    def stage_zyx(u, stage):
+        def column(d):
+            n = wrap(x + d, NX)
+            return wbuf.at[u, :, n // 2, core, :, n % 2]
+
+        def half(d, h):
+            n = wrap(x + d, NX)
+            return wbuf.at[u, pl.ds(2 * h, 2), n // 2, core, :, n % 2]
+
+        if stage == 0:
+            spread(u, 0, element(u), at_z, NZ)
+        if stage == 1:
+            got(u, 0)
+            spread(u, 1, wbuf.at[u, y, xh, core, :, xl], at_y, NY)
+        if stage == 2:
+            got(u, 1)
+            send(u, "r1", half(0, 0), at_x(1))
+            send(u, "l1", half(0, 1), at_x(3))
+            send(u, "r2", half(0, 1), at_x(1))
+            send(u, "l2", half(0, 0), at_x(3))
+            share(u, column(0))
+        if stage == 3:
+            got(u, "r1")
+            send(u, "far", half(-1, 0), at_x(1))
+            got(u, "l1")
+            send(u, "far", half(1, 1), at_x(3))
+            got(u, "r2")
+            share(u, column(-1))
+            got(u, "l2")
+            share(u, column(1))
+        if stage == 4:
+            got(u, "far")
+            share(u, column(2))
+
+    def stage_xyz(u, stage):
+        def group(d):
+            return wbuf.at[u, :, :, core, wrap(z + d, NZ)]
+
+        def half(d, h):
+            return wbuf.at[u, pl.ds(2 * h, 2), :, core, wrap(z + d, NZ)]
+
+        if stage == 0:
+            spread(u, 0, element(u), at_x, NX)
+        if stage == 1:
+            got(u, 0)
+            spread(u, 1, wbuf.at[u, y, :, core, z], at_y, NY)
+        if stage == 2:
+            got(u, 1)
+            send(u, "r2", group(0), at_z(2))
+            send(u, "l2", group(0), at_z(6))
+            send(u, "r1", group(0), at_z(1))
+            send(u, "l1", group(0), at_z(7))
+            share(u, group(0))
+        if stage == 3:
+            got(u, "r2")
+            send(u, "far", half(-2, 0), at_z(2))
+            send(u, "far", group(-2), at_z(1))
+            got(u, "l2")
+            send(u, "far", half(2, 1), at_z(6))
+            send(u, "far", group(2), at_z(7))
+            got(u, "r1")
+            got(u, "l1")
+            for d in (-2, -1, 1, 2):
+                share(u, group(d))
+        if stage == 4:
+            got(u, "far")
+            for d in (-3, 3, 4):
+                share(u, group(d))
 
     def gather_stage(u, stage):
-        if stage < 0 or stage >= STAGES:
-            return
-        if ORDERS[u] == "zx":
-            if stage <= 4:
-                ring_z(u, lambda u, n: element(u, x, n), stage)
-            if stage == 4:
-                send(u, 7, "xr1", column(u, x, 0, NZ), at_x(1))
-                send(u, 8, "xl1", column(u, x, 0, NZ), at_x(3))
-            if stage == 5:
-                got(u, "xr1")
-                send(u, 9, "xr2", column(u, x - 1, 0, 4), at_x(1))
-                got(u, "xl1")
-                send(u, 10, "xl2", column(u, x + 1, 4, 4), at_x(3))
-            if stage == 6:
-                got(u, "xr2")
-                got(u, "xl2")
-                share(u)
-        else:
-            if stage == 0:
-                send(u, 7, "xr1", element(u, x, z), at_x(1))
-                send(u, 8, "xl1", element(u, x, z), at_x(3))
-            if stage == 1:
-                got(u, "xr1")
-                send(u, 9, "xr2", part(u, x - 1, 0), at_x(1))
-                got(u, "xl1")
-                send(u, 10, "xl2", part(u, x + 1, 512), at_x(3))
-            if stage == 2:
-                got(u, "xr2")
-                got(u, "xl2")
-            if 2 <= stage <= 6:
-                ring_z(u, group, stage - 2)
-            if stage == 6:
-                share(u)
-        if stage == 7:
-            got(u, "s")
+        if 0 <= stage < STAGES:
+            {"zxy": stage_zxy, "zyx": stage_zyx, "xyz": stage_xyz}[ORDERS[u]](u, stage)
+        if stage == 5:
+            got(u, "share")
 
     clock = [0]
 
@@ -231,7 +290,7 @@
         rolls[which, i].wait_recv()
         return roll_r[which, i, pl.ds(0, QUARTER), :].astype(F32)
 
-    for which in range(3):
+    for which in range(4):
         for i in range(3):
             roll_s[which, i, pl.ds(32, 16), :] = jnp.zeros((16, D), BF16)
     roll_out(0, go_f, False)
@@ -309,25 +368,29 @@
     even = jnp.where(iota((1, 128), 1) < 64, 1.0, 0.0).astype(BF16)
     masks = (even, (1.0 - even.astype(F32)).astype(BF16))
 
-    def weight(u, first):
-        return wbuf[u, :, :, :, :, :, pl.ds(first, BLOCK)].reshape(D, BLOCK)
-
-    def weight_rows(u, block):
-        return wbuf[u, block // 2, block % 2].reshape(BLOCK, D)
+    def weight(u, block):
+        return wbuf[u, block].reshape(D, BLOCK)
+
+    def times_rows(left, u, block):
+        result = None
+        for c in range(4):
+            term = dot_t(left(c), wbuf[u, c, block // 2, block % 2].reshape(BLOCK, BLOCK))
+            result = term if result is None else result + term
+        return result
 
     def project(which):
         for u in range(3):
             def step(i, _):
                 first = pl.multiple_of(i * BLOCK, BLOCK)
-                result = dot(norm_buf[...], weight(which * 4 + u, first))
+                result = dot(norm_buf[...], weight(which * 4 + u, i))
                 qkv[which, :, pl.ds(pl.multiple_of(u * D + first, BLOCK), BLOCK)] = result.astype(BF16)
                 return 0
-            lax.fori_loop(0, D // BLOCK, step, 0)
+            lax.fori_loop(0, D // BLOCK, step, 0, unroll=4)
 
     def lanes(i, offset=0):
         return pl.ds(pl.multiple_of(offset + i * 128, 128), 128)
 
-    def attend(which):
+    def attend(which, first=0, last=HEADS // 2):
         def step(i, _):
             q2 = qkv[which, :, lanes(i)]
             k2 = qkv[which, :, lanes(i, D)]
@@ -344,9 +407,9 @@
                 mixed = term if mixed is None else mixed + term
             att_stack[which, i // 2, pl.ds(0, TOK), lanes(i % 2)] = mixed.astype(BF16)
             return 0
-        lax.fori_loop(0, HEADS // 2, step, 0)
-
-    def attend_back(which):
+        lax.fori_loop(first, last, step, 0, unroll=4)
+
+    def attend_back(which, first=0, last=HEADS // 2):
         def step(i, _):
             q2 = qkv[which, :, lanes(i)]
             k2 = qkv[which, :, lanes(i, D)]
@@ -370,18 +433,20 @@
             dqkv[:, lanes(i, D)] = dk.astype(BF16)
             dqkv[:, lanes(i, 2 * D)] = dv.astype(BF16)
             return 0
-        lax.fori_loop(0, HEADS // 2, step, 0)
-
-    def att_grad(which):
+        lax.fori_loop(first, last, step, 0, unroll=4)
+
+    def att_grad(source, which):
         for b in range(4):
-            datt[:, pl.ds(b * BLOCK, BLOCK)] = dot_t(
-                g_stack[which, pl.ds(0, TOK), :], weight_rows(which * 4 + 3, b)).astype(BF16)
+            datt[:, pl.ds(b * BLOCK, BLOCK)] = times_rows(
+                lambda c: source[pl.ds(0, TOK), pl.ds(c * BLOCK, BLOCK)],
+                which * 4 + 3, b).astype(BF16)
 
     def normed_grad(which):
         for b in range(4):
             result = None
             for u in range(3):
-                term = dot_t(dqkv[:, pl.ds(u * D, D)], weight_rows(which * 4 + u, b))
+                term = times_rows(
+                    lambda c: dqkv[:, pl.ds(u * D + c * BLOCK, BLOCK)], which * 4 + u, b)
                 result = term if result is None else result + term
             tmp_f[:, pl.ds(b * BLOCK, BLOCK)] = result.astype(BF16).astype(F32)
 
@@ -400,64 +465,114 @@
     def send_grad(m):
         to_sibling((m, 2), m * 3 + 2, g_stack.at[m, pl.ds(0, TOK)], g_stack.at[m, pl.ds(TOK, TOK)])
 
-    xflights, zflights, yflights = {}, {}, {}
-
-    def reduce_x(m):
-        for k in range(3):
-            sibs[m, k].wait_recv()
+    def turn_att(m):
         for h in range(2):
-            def step(i, _):
-                cols = pl.ds(pl.multiple_of(i * BLOCK, BLOCK), BLOCK)
-                result = t_dot(att_stack[m, h * 2 + core], g_stack[m, :, cols]).astype(BF16)
-                xs[m, h, :, :, :, cols] = result.reshape(NZ, 2, 16, BLOCK)
-                return 0
-            lax.fori_loop(0, D // BLOCK, step, 0)
+            sibs[m, h].wait_recv()
+            att_t[m, h] = att_stack[m, h * 2 + core].astype(F32).T.astype(BF16)
+
+    steps = {}
+
+    def ship(m, name, k, src, dst, device):
+        c = copy(src, dst, red_send.at[m, k], red_recv.at[m, k], device)
+        c.start()
+        steps.setdefault((m, name), []).append(c)
+
+    def landed(m, name):
+        for c in steps[m, name]:
+            c.wait_recv()
+
+    def product(m, h, cols):
+        return dot(att_t[m, h], g_stack[m, :, cols])
+
+    def early_product():
+        sibs[0, 2].wait_recv()
+        for h in range(2):
+            for c in range(4):
+                cols = pl.ds(c * BLOCK, BLOCK)
+                early[h, :, cols] = product(0, h, cols)
+
+    def reduce_1(m):
+        sibs[2 if m == 0 else 1, 2].wait_recv()
+        for h in range(2):
+            for c in range(4):
+                cols = pl.ds(c * BLOCK, BLOCK)
+                if m == 0:
+                    value = product(2, h, cols) + early[h, :, cols]
+                else:
+                    value = product(1, h, cols)
+                value = value.astype(BF16)
+                if c < 2:
+                    xs[m, h, :, :, :, cols] = value.reshape(NZ, 2, 16, BLOCK)
+                else:
+                    for q in range(2):
+                        vs[m, (c - 2) * 2 + q, h] = value[:, q * 128:(q + 1) * 128].reshape(
+                            NZ, 2, 16, 128)
         for d in (2, 1, 3):
             target = (x + d) % NX
-            c = copy(xs.at[m, target // 2, :, target % 2], xr.at[m, d - 1],
-                     x_send.at[m, d - 1], x_recv.at[m, d - 1], at_x(d))
-            c.start()
-            xflights[m, d] = c
-
-    def reduce_z(m):
-        for d in range(1, NX):
-            xflights[m, d].wait_recv()
-
-        def step(i, _):
-            value = xs[m, xh, i, xl].astype(F32)
-            for d in range(NX - 1):
-                value = value + xr[m, d, i].astype(F32)
-            zs[m, i] = value.astype(BF16)
-            return 0
-        lax.fori_loop(0, NZ, step, 0)
+            ship(m, "xx", d - 1, xs.at[m, target // 2, :, target % 2], xr.at[m, d - 1], at_x(d))
+            ship(m, "vy", 2 + d, vs.at[m, (y + d) % NY], vr.at[m, d - 1], at_y(d))
+
+    def reduce_2(m):
+        landed(m, "xx")
+        value = xs[m, xh, :, xl].astype(F32)
+        for d in range(NX - 1):
+            value = value + xr[m, d].astype(F32)
+        zs[m] = value.astype(BF16)
         for d in (4, 3, 5, 2, 6, 1, 7):
-            c = copy(zs.at[m, (z + d) % NZ], zr.at[m, d - 1],
-                     z_send.at[m, d - 1], z_recv.at[m, d - 1], at_z(d))
-            c.start()
-            zflights[m, d] = c
-
-    def reduce_y(m):
-        for d in range(1, NZ):
-            zflights[m, d].wait_recv()
+            ship(m, "xz", 5 + d, zs.at[m, (z + d) % NZ], zr.at[m, d - 1], at_z(d))
+        landed(m, "vy")
+        value = vs[m, y].astype(F32)
+        for d in range(NY - 1):
+            value = value + vr[m, d].astype(F32)
+        ws[m] = value.astype(BF16)
+        for d in (2, 1, 3):
+            target = (x + d) % NX
+            ship(m, "vx", 12 + d, ws.at[m, target // 2, :, target % 2], wr.at[m, d - 1], at_x(d))
+
+    def reduce_3(m):
+        landed(m, "vx")
+        value = ws[m, xh, :, xl].astype(F32)
+        for d in range(NX - 1):
+            value = value + wr[m, d].astype(F32)
+        us[m] = value.astype(BF16)
+        for d in (4, 3, 5, 2, 6, 1, 7):
+            ship(m, "vz", 15 + d, us.at[m, (z + d) % NZ], ur.at[m, d - 1], at_z(d))
+        landed(m, "xz")
         value = zs[m, z].astype(F32)
         for d in range(NZ - 1):
             value = value + zr[m, d].astype(F32)
         ys[m, y] = value.astype(BF16)
         for d in range(1, NY):
-            c = copy(ys.at[m, y], ys.at[m, y], y_send.at[m, d - 1], y_recv.at[m, d - 1], at_y(d))
-            c.start()
-            yflights[m, d] = c
+            ship(m, "xy", 22 + d, ys.at[m, y], ys.at[m, y], at_y(d))
+
+    def reduce_4(m):
+        landed(m, "vz")
+        value = us[m, z].astype(F32)
+        for d in range(NZ - 1):
+            value = value + ur[m, d].astype(F32)
+        os[m, y] = value.astype(BF16)
+        for d in range(1, NY):
+            ship(m, "vo", 25 + d, os.at[m, y], os.at[m, y], at_y(d))
 
     def reduce_end(m, target):
-        for d in range(1, NY):
-            yflights[m, d].wait_recv()
+        landed(m, "xy")
         value = ys[m, 0].astype(F32)
         for i in range(1, NY):
             value = value + ys[m, i].astype(F32)
-        target[...] = value
+        target[:, pl.ds(0, 512)] = value
+        landed(m, "vo")
+        for i in range(NY):
+            target[:, pl.ds(512 + i * 128, 128)] = os[m, i].astype(F32)
 
     unit, _ = norm_parts(tok_f[...])
     norm_buf[...] = (unit * gain1_ref[...]).astype(BF16)
+    g_stack[0, pl.ds(0, TOK), :] = go_f[...].astype(BF16)
+    send_grad(0)
+    sh_f[pl.ds(0, QUARTER), :] = go_f[pl.ds(3 * QUARTER, QUARTER), :]
+    for i in range(3):
+        sh_f[pl.ds((i + 1) * QUARTER, QUARTER), :] = roll_in(0, i)
+    g_stack[1, pl.ds(0, TOK), :] = sh_f[...].astype(BF16)
+    send_grad(1)
     gather_until((0, 1, 2))
     project(0)
     gather_turn()
@@ -469,52 +584,67 @@
         result = tok_f[:, cols]
         for h in range(4):
             result = result + dot(att_stack[0, h, pl.ds(0, TOK), :],
-                                  wbuf[3, h // 2, h % 2, :, :, :, cols].reshape(BLOCK, BLOCK))
+                                  wbuf[3, b, h // 2, h % 2].reshape(BLOCK, BLOCK))
         mid_f[:, cols] = result.astype(BF16).astype(F32)
     roll_out(1, mid_f, False)
-    sh_f[pl.ds(0, QUARTER), :] = go_f[pl.ds(3 * QUARTER, QUARTER), :]
-    for i in range(3):
-        sh_f[pl.ds((i + 1) * QUARTER, QUARTER), :] = roll_in(0, i)
-    g_stack[1, pl.ds(0, TOK), :] = sh_f[...].astype(BF16)
-    send_grad(1)
-    gather_until(range(8))
-    att_grad(1)
+    for h in range(4):
+        tmp_f[:, pl.ds(h * BLOCK, BLOCK)] = att_stack[0, h, pl.ds(0, TOK), :].astype(F32)
+    roll_out(3, tmp_f, False)
+    turn_att(0)
+    early_product()
     sh_f[pl.ds(0, QUARTER), :] = mid_f[pl.ds(3 * QUARTER, QUARTER), :]
     for i in range(3):
         sh_f[pl.ds((i + 1) * QUARTER, QUARTER), :] = roll_in(1, i)
     unit, _ = norm_parts(sh_f[...])
     norm_buf[...] = (unit * gain2_ref[...]).astype(BF16)
+    mid_f[pl.ds(0, QUARTER), :] = tmp_f[pl.ds(3 * QUARTER, QUARTER), :]
+    for i in range(3):
+        mid_f[pl.ds((i + 1) * QUARTER, QUARTER), :] = roll_in(3, i)
+    for h in range(4):
+        att_stack[2, h, pl.ds(0, TOK), :] = mid_f[:, pl.ds(h * BLOCK, BLOCK)].astype(BF16)
+    send_att(2)
+    gather_until(range(8))
+    att_grad(g_stack.at[1], 1)
     project(1)
     attend(1)
     send_att(1)
+    turn_att(2)
     attend_back(1)
-    reduce_x(1)
+    turn_att(1)
+    reduce_1(1)
     normed_grad(1)
     mid_f[...] = norm_back(sh_f[...], gain2_ref[...], tmp_f[...])
+    g_stack[2, pl.ds(0, TOK), :] = mid_f[...].astype(BF16)
+    send_grad(2)
     roll_out(2, mid_f, True)
+    reduce_1(0)
     sh_f[pl.ds(3 * QUARTER, QUARTER), :] = mid_f[pl.ds(0, QUARTER), :].astype(BF16).astype(F32)
-    reduce_z(1)
     for i, quarter in enumerate((2, 1, 0)):
         sh_f[pl.ds(quarter * QUARTER, QUARTER), :] = roll_in(2, i)
     mid_f[...] = (go_f[...] + sh_f[...]).astype(BF16).astype(F32)
-    g_stack[0, pl.ds(0, TOK), :] = mid_f[...].astype(BF16)
-    send_grad(0)
-    att_grad(0)
-    reduce_x(0)
-    attend_back(0)
-    reduce_y(1)
+    norm_buf[...] = mid_f[...].astype(BF16)
+    att_grad(norm_buf, 0)
+    reduce_2(1)
+    attend_back(0, 0, 4)
+    reduce_2(0)
+    attend_back(0, 4, 8)
+    reduce_3(1)
     normed_grad(0)
-    reduce_z(0)
+    reduce_3(0)
     sh_f[...] = mid_f[...] + norm_back(tok_f[...], gain1_ref[...], tmp_f[...]).astype(BF16).astype(F32)
     for r in range(WIN):
         rows = jnp.concatenate(
             [sh_f[pl.ds(r * HALF, HALF), :], sh_f[pl.ds(72 + r * HALF, HALF), :]], axis=0)
         out_ref[0, r] = rows.astype(BF16)
+    reduce_4(1)
+    reduce_4(0)
     reduce_end(1, og2_ref)
-    reduce_y(0)
     reduce_end(0, og1_ref)
-    for group_of in (flights, rolls, sibs, xflights, zflights, yflights):
+    for group_of in (flights, rolls, sibs):
         for c in group_of.values():
+            c.wait_send()
+    for some in steps.values():
+        for c in some:
             c.wait_send()
 
 
@@ -537,7 +667,7 @@
         in_specs=[vmem] * 4 + [hbm] * 4 + [vmem] * 3,
         out_specs=(vmem, vmem, vmem),
         scratch_shapes=[
-            pltpu.VMEM((8, 2, 2, NZ, 2, 16, D), BF16),
+            pltpu.VMEM((8, NY, 2, 2, NZ, 2, 16, BLOCK), BF16),
             pltpu.VMEM((2 * HEADS, TOK, TOK), F32),
             pltpu.VMEM((16, 512), jnp.int32),
             pltpu.VMEM((WIN, 2 * HEADS, 512), F32),
@@ -553,22 +683,29 @@
             pltpu.VMEM((TOK, D), F32),
             pltpu.VMEM((TOK, D), F32),
             pltpu.VMEM((TOK, D), F32),
-            pltpu.VMEM((2, 2 * TOK, D), BF16),
-            pltpu.VMEM((2, 4, 2 * TOK, BLOCK), BF16),
-            pltpu.VMEM((3, 3, 48, D), BF16),
-            pltpu.VMEM((3, 3, 48, D), BF16),
-            pltpu.VMEM((2, 2, NZ, 2, 16, D), BF16),
-            pltpu.VMEM((2, NX - 1, NZ, 16, D), BF16),
-            pltpu.VMEM((2, NZ, 16, D), BF16),
-            pltpu.VMEM((2, NZ - 1, 16, D), BF16),
-            pltpu.VMEM((2, NY, 16, D), BF16),
+            pltpu.VMEM((3, 2 * TOK, D), BF16),
+            pltpu.VMEM((3, 4, 2 * TOK, BLOCK), BF16),
+            pltpu.VMEM((4, 3, 48, D), BF16),
+            pltpu.VMEM((4, 3, 48, D), BF16),
+            pltpu.VMEM((3, 2, BLOCK, 2 * TOK), BF16),
+            pltpu.VMEM((2, BLOCK, D), F32),
+            pltpu.VMEM((2, 2, NZ, 2, 16, 512), BF16),
+            pltpu.VMEM((2, NX - 1, NZ, 16, 512), BF16),
+            pltpu.VMEM((2, NZ, 16, 512), BF16),
+            pltpu.VMEM((2, NZ - 1, 16, 512), BF16),
+            pltpu.VMEM((2, NY, 16, 512), BF16),
+            pltpu.VMEM((2, NY, 2, NZ, 2, 16, 128), BF16),
+            pltpu.VMEM((2, NY - 1, 2, NZ, 2, 16, 128), BF16),
+            pltpu.VMEM((2, 2, NZ, 2, 16, 128), BF16),
+            pltpu.VMEM((2, NX - 1, NZ, 16, 128), BF16),
+            pltpu.VMEM((2, NZ, 16, 128), BF16),
+            pltpu.VMEM((2, NZ - 1, 16, 128), BF16),
+            pltpu.VMEM((2, NY, 16, 128), BF16),
             dma((8,)),
-            dma((8, 12)), dma((8, 12)),
-            dma((3, 3)), dma((3, 3)),
-            dma((6,)), dma((6,)),
-            dma((2, NX - 1)), dma((2, NX - 1)),
-            dma((2, NZ - 1)), dma((2, NZ - 1)),
-            dma((2, NY - 1)), dma((2, NY - 1)),
+            dma((8, 24)), dma((8, 24)),
+            dma((4, 3)), dma((4, 3)),
+            dma((9,)), dma((9,)),
+            dma((2, 29)), dma((2, 29)),
         ],
         compiler_params=pltpu.CompilerParams(
             collective_id=0, has_side_effects=True, vmem_limit_bytes=56 * 1024 * 1024

time: 157 us -> 119 us (0.76)
  Pallas kernels: 150 us -> 112 us
    pallas_call x1, Pallas kernels: 150 us -> 112 us  [on_device(): pl.pallas_call(kernel, out_shape=(jax.ShapeDtypeStruct((1, WIN, WIN, D),...]
where the time goes in v2:
time: 119 us; the launch traced here: 118 us
  Pallas kernels  112 us (94%)
  local copies, waits for them, and re-layouts  3.93 us (3%)
    pallas_call x1, Pallas kernels, on_device(): pl.pallas_call(kernel, out_shape=(jax.ShapeDtypeStruct((1, WIN, WIN, D),...  112 us
    unnamed x7, local copies, waits for them, and re-layouts  3.29 us

profile of v2, /device:TPU:8, one launch (start us, length us, event | category | flops | bytes accessed | tf_op | source)
XLA Modules:
  0.0 117.6 jit_solution(277890175711674825)
XLA Ops:
  0.6 0.8 maximum_bitcast_fusion
  1.4 0.6 pad.4.tab_ref
  2.1 112.2 %window_blocks.1 = (bf16[1,12,12,1024]{3,2,1,0:T(8,128)(2,1)}, f32[16,1024]{1,0:T(8,128)}, f32[16,1024]{1,0:T(8,128)}) custom-call(bf16[1,12,12,1024]{3,2,1,0:T(8,128)(2,1)} %tokens_ref.1, bf16[1,12,12,1024]{3,2,1,0:T(8,128)(2,1)} %grad_ref.1, f32[1,1024]{1,0:T(1,128)} %bitcast.4, f32[1,1024]{1,0:T(1,128)} %bitcast.5, bf16[16,3072]{1,0:T(8,128)(2,1)} %wq1_ref.1, ...), custom_call_target="tpu_custom_call" | custom-call | tf_op jit(solution)/shard_map/window_blocks/pallas_call | solution.py:660
  114.3 0.0 copy-start.1
  114.3 1.8 %copy.18 = bf16[1,12,12,1024]{3,2,1,0:T(8,128)(2,1)} copy(bf16[1,12,12,1024]{3,2,1,0:T(8,128)(2,1)} %get-tuple-element.6) | data formatting | bytes 589824
  116.1 0.0 copy-done.1
  116.1 0.0 copy-start
  116.1 0.6 copy.19
  116.7 0.2 copy-done
  116.9 0.6 copy.20
Async XLA Ops:
  114.3 1.8 %copy-start.1 = (f32[16,1024]{1,0:T(8,128)S(1)}, f32[16,1024]{1,0:T(8,128)}, u32[]{:S(2)}) copy-start(f32[16,1024]{1,0:T(8,128)} %get-tuple-element.7) | copy-start | bytes 196612
  116.1 0.9 copy-start

commit v3 on v2

--- a/solution.py
+++ b/solution.py
@@ -21,8 +21,7 @@
 BF16 = jnp.bfloat16
 
 ORDERS = ("zxy", "zyx", "xyz", "zxy", "zyx", "zxy", "xyz", "zyx")
-STARTS = (0, 0, 0, 1, 1, 2, 2, 2)
-STAGES = 6
+STAGES = 7
 
 
 def dot(a, b):
@@ -43,6 +42,10 @@
 
 def over_six(n):
     return (n * 10923) >> 16
+
+
+def qkv_column(n):
+    return (n % 3) * D + (n // 3) * BLOCK
 
 
 def norm_parts(x):
@@ -61,12 +64,13 @@
 
 def kernel(
     tokens_ref, grad_ref, gain1_ref, gain2_ref, wq1_ref, wo1_ref, wq2_ref, wo2_ref,
-    tab_ref, rel_ref, cls_ref,
+    bias1_ref, bias2_ref, rel_in, cls_in,
     out_ref, og1_ref, og2_ref,
+    tokens_v, grad_v, bias1_v, bias2_v, rel_ref, cls_ref, tab,
     wbuf, bias, idx_u, u_raw, u_ref, same, probs, qkv, dqkv, norm_buf, datt,
     tok_f, go_f, mid_f, sh_f, tmp_f, g_stack, att_stack, roll_s, roll_r,
-    att_t, early, xs, xr, zs, zr, ys, vs, vr, ws, wr, us, ur, os,
-    w_local, w_send, w_recv, roll_send, roll_recv, sib_send, sib_recv, red_send, red_recv,
+    partial, att_t, early, xs, xr, zs, zr, ys, vs, vr, ws, wr, us, ur, os,
+    load_sem, w_local, w_send, w_recv, roll_send, roll_recv, sib_send, sib_recv, red_send, red_recv,
 ):
     lat, lon, y = lax.axis_index("lat"), lax.axis_index("lon"), lax.axis_index("rep")
     xh, core = lat // 2, lat % 2
@@ -95,24 +99,34 @@
             device_id=device, device_id_type=MESH,
         )
 
-    local = []
-    for u in range(8):
-        source = (wq1_ref, wo1_ref, wq2_ref, wo2_ref)[(u // 4) * 2 + (u % 4) // 3]
-        column = (u % 4) * D if u % 4 < 3 else 0
-        local.append(
-            pltpu.make_async_copy(
-                source.at[:, pl.ds(pl.multiple_of(column + y * BLOCK, BLOCK), BLOCK)],
-                wbuf.at[u, y, xh, core, z, xl], w_local.at[u],
-            )
-        )
-        local[-1].start()
-
     barrier = pltpu.get_barrier_semaphore()
     partners = [at_z(d) for d in range(1, NZ)] + [at_x(d) for d in range(1, NX)]
     partners += [at_y(d) for d in range(1, NY)] + [sibling]
     partners += [at_roll(*s) for s in ((1, 0), (-1, 0), (0, 1), (0, -1), (1, 1), (-1, -1))]
     for partner in partners:
         pl.semaphore_signal(barrier, inc=1, device_id=partner, device_id_type=MESH)
+    local = []
+    for u in range(8):
+        source = (wq1_ref, wo1_ref, wq2_ref, wo2_ref)[(u // 4) * 2 + (u % 4) // 3]
+        n = (u % 4) * 4 + y
+        column = qkv_column(n) if u % 4 < 3 else y * BLOCK
+        local.append(
+            pltpu.make_async_copy(
+                source.at[:, pl.ds(pl.multiple_of(column, BLOCK), BLOCK)],
+                wbuf.at[u, y, xh, core, z, xl], w_local.at[u],
+            )
+        )
+        local[-1].start()
+
+    loads = [
+        pltpu.make_async_copy(source, target, load_sem.at[i])
+        for i, (source, target) in enumerate((
+            (grad_ref, grad_v), (rel_in, rel_ref), (tokens_ref, tokens_v),
+            (bias1_ref, bias1_v), (bias2_ref, bias2_v), (cls_in, cls_ref)))
+    ]
+    for c in loads:
+        c.start()
+
     pl.semaphore_wait(barrier, len(partners))
     for c in local:
         c.wait()
@@ -170,11 +184,12 @@
             send(u, "far", half(-1, 0), at_y(1))
             got(u, "l1")
             send(u, "far", half(1, 1), at_y(3))
+        if stage == 4:
             got(u, "r2")
             share(u, plane(-1))
             got(u, "l2")
             share(u, plane(1))
-        if stage == 4:
+        if stage == 5:
             got(u, "far")
             share(u, plane(2))
 
@@ -204,11 +219,12 @@
             send(u, "far", half(-1, 0), at_x(1))
             got(u, "l1")
             send(u, "far", half(1, 1), at_x(3))
+        if stage == 4:
             got(u, "r2")
             share(u, column(-1))
             got(u, "l2")
             share(u, column(1))
-        if stage == 4:
+        if stage == 5:
             got(u, "far")
             share(u, column(2))
 
@@ -238,11 +254,12 @@
             got(u, "l2")
             send(u, "far", half(2, 1), at_z(6))
             send(u, "far", group(2), at_z(7))
+        if stage == 4:
             got(u, "r1")
             got(u, "l1")
             for d in (-2, -1, 1, 2):
                 share(u, group(d))
-        if stage == 4:
+        if stage == 5:
             got(u, "far")
             for d in (-3, 3, 4):
                 share(u, group(d))
@@ -250,24 +267,19 @@
     def gather_stage(u, stage):
         if 0 <= stage < STAGES:
             {"zxy": stage_zxy, "zyx": stage_zyx, "xyz": stage_xyz}[ORDERS[u]](u, stage)
-        if stage == 5:
+        if stage == 6:
             got(u, "share")
 
-    clock = [0]
-
-    def gather_turn():
-        for u in range(8):
-            gather_stage(u, clock[0] - STARTS[u])
-        clock[0] += 1
-
-    def gather_until(units):
-        while clock[0] < max(STARTS[u] for u in units) + STAGES:
-            gather_turn()
-
-    gather_turn()
+    def gather(stage, *units):
+        for u in units:
+            gather_stage(u, stage)
+
+    gather(0, 0, 1, 2, 3, 4, 5, 6, 7)
+    for c in loads:
+        c.wait()
 
     for r in range(WIN):
-        for source, target in ((tokens_ref, tok_f), (grad_ref, go_f)):
+        for source, target in ((tokens_v, tok_f), (grad_v, go_f)):
             rows = source[0, r].astype(F32)
             target[pl.ds(r * HALF, HALF), :] = rows[:HALF]
             target[pl.ds(72 + r * HALF, HALF), :] = rows[HALF:]
@@ -279,8 +291,9 @@
         places = ((1, (to, 0)), (2, (0, to)), (3, (to, to))) if back else (
             (2, (to, 0)), (1, (0, to)), (0, (to, to)))
         for i, (quarter, shift) in enumerate(places):
-            roll_s[which, i, pl.ds(0, QUARTER), :] = source[
-                pl.ds(quarter * QUARTER, QUARTER), :].astype(BF16)
+            rows = source[pl.ds(quarter * QUARTER, QUARTER), :]
+            roll_s[which, i] = jnp.concatenate(
+                [rows[:, c * BLOCK:(c + 1) * BLOCK] for c in range(4)], axis=0).astype(BF16)
             c = copy(roll_s.at[which, i], roll_r.at[which, i],
                      roll_send.at[which, i], roll_recv.at[which, i], at_roll(*shift))
             c.start()
@@ -288,13 +301,11 @@
 
     def roll_in(which, i):
         rolls[which, i].wait_recv()
-        return roll_r[which, i, pl.ds(0, QUARTER), :].astype(F32)
-
-    for which in range(4):
-        for i in range(3):
-            roll_s[which, i, pl.ds(32, 16), :] = jnp.zeros((16, D), BF16)
+        rows = roll_r[which, i].astype(F32)
+        return jnp.concatenate(
+            [rows[c * QUARTER:(c + 1) * QUARTER] for c in range(4)], axis=1)
+
     roll_out(0, go_f, False)
-    gather_turn()
 
     k_of = iota((TOK, 512), 0)
     lane = iota((TOK, 512), 1)
@@ -313,9 +324,13 @@
     high_b = dot((rel_ref[pl.ds(0, WIN), :] >> 4).astype(F32).astype(BF16), pick_b)
     low_b = dot((rel_ref[pl.ds(0, WIN), :] & 15).astype(F32).astype(BF16), pick_b)
     idx_u[pl.ds(0, WIN), :] = ((high_a + high_b) * 16.0 + low_a + low_b).astype(jnp.int32)
-    gather_turn()
-
-    table = tab_ref[...]
+    gather(1, 0, 1, 2)
+
+    tab[...] = jnp.zeros_like(tab)
+    entries = bias1_v.shape[1]
+    tab[pl.ds(0, HEADS), pl.ds(0, entries)] = bias1_v[...]
+    tab[pl.ds(HEADS, HEADS), pl.ds(0, entries)] = bias2_v[...]
+    table = tab[...]
     t_high = table.astype(BF16)
     rest = table - t_high.astype(F32)
     t_mid = rest.astype(BF16)
@@ -330,7 +345,8 @@
         return 0
 
     lax.fori_loop(0, WIN, choose, 0)
-    gather_turn()
+    gather(2, 0, 1, 2)
+    gather(1, 3, 4, 6, 5, 7)
     for th in range(2 * HEADS):
         rows = u_raw[:, th, :]
         u_ref[th, pl.ds(0, HALF), :] = rows[:HALF]
@@ -349,7 +365,6 @@
         return 0
 
     lax.fori_loop(0, HEADS, slide, 0)
-    gather_turn()
 
     n = iota((TOK, WIN), 0)
     right_half = (n >= 72).astype(jnp.int32)
@@ -363,6 +378,8 @@
     member = jnp.where(iota((TOK, 128), 1) == label.astype(jnp.int32), 1.0, 0.0).astype(BF16)
     same[...] = dot_t(member, member)
 
+    gather(3, 0, 1)
+    gather(2, 3, 4)
     lax.fori_loop(HEADS, 2 * HEADS, slide, 0)
 
     even = jnp.where(iota((1, 128), 1) < 64, 1.0, 0.0).astype(BF16)
@@ -378,14 +395,20 @@
             result = term if result is None else result + term
         return result
 
-    def project(which):
-        for u in range(3):
-            def step(i, _):
-                first = pl.multiple_of(i * BLOCK, BLOCK)
-                result = dot(norm_buf[...], weight(which * 4 + u, i))
-                qkv[which, :, pl.ds(pl.multiple_of(u * D + first, BLOCK), BLOCK)] = result.astype(BF16)
-                return 0
-            lax.fori_loop(0, D // BLOCK, step, 0, unroll=4)
+    def project(which, own, *parts_of):
+        half = core if own else other
+        for u in parts_of:
+            for i in range(4):
+                cols = pl.ds(i * BLOCK, BLOCK)
+                result = None if own else partial[u, :, cols]
+                for h in range(2):
+                    rows = pl.ds(pl.multiple_of(h * 512 + half * BLOCK, BLOCK), BLOCK)
+                    term = dot(norm_buf[:, rows], wbuf[which * 4 + u, i, h, half].reshape(BLOCK, BLOCK))
+                    result = term if result is None else result + term
+                if own:
+                    partial[u, :, cols] = result
+                else:
+                    qkv[which, :, pl.ds(qkv_column(u * 4 + i), BLOCK)] = result.astype(BF16)
 
     def lanes(i, offset=0):
         return pl.ds(pl.multiple_of(offset + i * 128, 128), 128)
@@ -446,7 +469,7 @@
             result = None
             for u in range(3):
                 term = times_rows(
-                    lambda c: dqkv[:, pl.ds(u * D + c * BLOCK, BLOCK)], which * 4 + u, b)
+                    lambda c: dqkv[:, pl.ds(qkv_column(u * 4 + c), BLOCK)], which * 4 + u, b)
                 result = term if result is None else result + term
             tmp_f[:, pl.ds(b * BLOCK, BLOCK)] = result.astype(BF16).astype(F32)
 
@@ -564,6 +587,9 @@
         for i in range(NY):
             target[:, pl.ds(512 + i * 128, 128)] = os[m, i].astype(F32)
 
+    gather(3, 2)
+    gather(2, 6)
+    gather(4, 0, 1)
     unit, _ = norm_parts(tok_f[...])
     norm_buf[...] = (unit * gain1_ref[...]).astype(BF16)
     g_stack[0, pl.ds(0, TOK), :] = go_f[...].astype(BF16)
@@ -573,12 +599,25 @@
         sh_f[pl.ds((i + 1) * QUARTER, QUARTER), :] = roll_in(0, i)
     g_stack[1, pl.ds(0, TOK), :] = sh_f[...].astype(BF16)
     send_grad(1)
-    gather_until((0, 1, 2))
-    project(0)
-    gather_turn()
-    attend(0)
+    gather(5, 0, 1)
+    gather(4, 2)
+    project(0, True, 0, 1)
+    gather(3, 3, 4)
+    gather(2, 5, 7)
+    gather(6, 0, 1)
+    project(0, False, 0, 1)
+    gather(5, 2)
+    attend(0, 0, 4)
+    gather(4, 3, 4)
+    project(0, True, 2)
+    gather(6, 2)
+    project(0, False, 2)
+    gather(5, 3, 4)
+    attend(0, 4, 8)
     send_att(0)
-    gather_until((3,))
+    gather(3, 5, 7)
+    gather(3, 6)
+    gather(6, 3)
     for b in range(4):
         cols = pl.ds(b * BLOCK, BLOCK)
         result = tok_f[:, cols]
@@ -587,31 +626,45 @@
                                   wbuf[3, b, h // 2, h % 2].reshape(BLOCK, BLOCK))
         mid_f[:, cols] = result.astype(BF16).astype(F32)
     roll_out(1, mid_f, False)
-    for h in range(4):
-        tmp_f[:, pl.ds(h * BLOCK, BLOCK)] = att_stack[0, h, pl.ds(0, TOK), :].astype(F32)
-    roll_out(3, tmp_f, False)
     turn_att(0)
+    gather(4, 5, 7)
+    gather(4, 6)
     early_product()
+    gather(6, 4)
+    gather(5, 5, 7)
     sh_f[pl.ds(0, QUARTER), :] = mid_f[pl.ds(3 * QUARTER, QUARTER), :]
     for i in range(3):
         sh_f[pl.ds((i + 1) * QUARTER, QUARTER), :] = roll_in(1, i)
     unit, _ = norm_parts(sh_f[...])
     norm_buf[...] = (unit * gain2_ref[...]).astype(BF16)
+    project(1, True, 0)
+    project(1, False, 0)
+    project(1, True, 1)
+    gather(6, 5)
+    project(1, False, 1)
+    gather(5, 6)
+    project(1, True, 2)
+    attend(1, 0, 4)
+    gather(6, 6)
+    project(1, False, 2)
+    attend(1, 4, 8)
+    send_att(1)
+    for h in range(4):
+        tmp_f[:, pl.ds(h * BLOCK, BLOCK)] = att_stack[0, h, pl.ds(0, TOK), :].astype(F32)
+    roll_out(3, tmp_f, False)
+    gather(6, 7)
+    att_grad(g_stack.at[1], 1)
+    attend_back(1, 0, 4)
+    turn_att(1)
+    reduce_1(1)
     mid_f[pl.ds(0, QUARTER), :] = tmp_f[pl.ds(3 * QUARTER, QUARTER), :]
     for i in range(3):
         mid_f[pl.ds((i + 1) * QUARTER, QUARTER), :] = roll_in(3, i)
     for h in range(4):
         att_stack[2, h, pl.ds(0, TOK), :] = mid_f[:, pl.ds(h * BLOCK, BLOCK)].astype(BF16)
     send_att(2)
-    gather_until(range(8))
-    att_grad(g_stack.at[1], 1)
-    project(1)
-    attend(1)
-    send_att(1)
+    attend_back(1, 4, 8)
     turn_att(2)
-    attend_back(1)
-    turn_att(1)
-    reduce_1(1)
     normed_grad(1)
     mid_f[...] = norm_back(sh_f[...], gain2_ref[...], tmp_f[...])
     g_stack[2, pl.ds(0, TOK), :] = mid_f[...].astype(BF16)
@@ -625,17 +678,16 @@
     norm_buf[...] = mid_f[...].astype(BF16)
     att_grad(norm_buf, 0)
     reduce_2(1)
-    attend_back(0, 0, 4)
-    reduce_2(0)
-    attend_back(0, 4, 8)
+    attend_back(0)
     reduce_3(1)
     normed_grad(0)
-    reduce_3(0)
+    reduce_2(0)
     sh_f[...] = mid_f[...] + norm_back(tok_f[...], gain1_ref[...], tmp_f[...]).astype(BF16).astype(F32)
     for r in range(WIN):
         rows = jnp.concatenate(
             [sh_f[pl.ds(r * HALF, HALF), :], sh_f[pl.ds(72 + r * HALF, HALF), :]], axis=0)
         out_ref[0, r] = rows.astype(BF16)
+    reduce_3(0)
     reduce_4(1)
     reduce_4(0)
     reduce_end(1, og2_ref)
@@ -652,8 +704,6 @@
     tokens, grad_out, first_gain, first_qkv_weight, first_out_weight, first_bias,
     second_gain, second_qkv_weight, second_out_weight, second_bias, rel_index, classes,
 ):
-    table = jnp.concatenate([first_bias, second_bias], axis=1).T
-    table = jnp.pad(table, ((0, 0), (0, TABLE - table.shape[1])))
     vmem = pl.BlockSpec(memory_space=pltpu.VMEM)
     hbm = pl.BlockSpec(memory_space=pl.ANY)
     dma = pltpu.SemaphoreType.DMA
@@ -664,9 +714,16 @@
             jax.ShapeDtypeStruct((16, D), F32),
             jax.ShapeDtypeStruct((16, D), F32),
         ),
-        in_specs=[vmem] * 4 + [hbm] * 4 + [vmem] * 3,
+        in_specs=[hbm] * 2 + [vmem] * 2 + [hbm] * 8,
         out_specs=(vmem, vmem, vmem),
         scratch_shapes=[
+            pltpu.VMEM((1, WIN, WIN, D), BF16),
+            pltpu.VMEM((1, WIN, WIN, D), BF16),
+            pltpu.VMEM(first_bias.shape[::-1], F32),
+            pltpu.VMEM(second_bias.shape[::-1], F32),
+            pltpu.VMEM((TOK, TOK), jnp.int32),
+            pltpu.VMEM((WIN, WIN), jnp.int32),
+            pltpu.VMEM((2 * HEADS, TABLE), F32),
             pltpu.VMEM((8, NY, 2, 2, NZ, 2, 16, BLOCK), BF16),
             pltpu.VMEM((2 * HEADS, TOK, TOK), F32),
             pltpu.VMEM((16, 512), jnp.int32),
@@ -685,8 +742,9 @@
             pltpu.VMEM((TOK, D), F32),
             pltpu.VMEM((3, 2 * TOK, D), BF16),
             pltpu.VMEM((3, 4, 2 * TOK, BLOCK), BF16),
-            pltpu.VMEM((4, 3, 48, D), BF16),
-            pltpu.VMEM((4, 3, 48, D), BF16),
+            pltpu.VMEM((4, 3, TOK, BLOCK), BF16),
+            pltpu.VMEM((4, 3, TOK, BLOCK), BF16),
+            pltpu.VMEM((3, TOK, D), F32),
             pltpu.VMEM((3, 2, BLOCK, 2 * TOK), BF16),
             pltpu.VMEM((2, BLOCK, D), F32),
             pltpu.VMEM((2, 2, NZ, 2, 16, 512), BF16),
@@ -701,6 +759,7 @@
             pltpu.VMEM((2, NZ, 16, 128), BF16),
             pltpu.VMEM((2, NZ - 1, 16, 128), BF16),
             pltpu.VMEM((2, NY, 16, 128), BF16),
+            dma((6,)),
             dma((8,)),
             dma((8, 24)), dma((8, 24)),
             dma((4, 3)), dma((4, 3)),
@@ -714,7 +773,7 @@
     )(
         tokens, grad_out, first_gain[None], second_gain[None],
         first_qkv_weight, first_out_weight, second_qkv_weight, second_out_weight,
-        table, rel_index, classes,
+        first_bias.T, second_bias.T, rel_index, classes,
     )
 
 

time: 119 us -> 110 us (0.924)
  Pallas kernels: 112 us -> 106 us
    pallas_call x1, Pallas kernels: 112 us -> 106 us  [on_device(): pl.pallas_call(kernel, out_shape=(jax.ShapeDtypeStruct((1, WIN, WIN, D),...]
where the time goes in v3:
time: 110 us; the launch traced here: 109 us
  Pallas kernels  106 us (96%)
  local copies, waits for them, and re-layouts  3.29 us (3%)
    pallas_call x1, Pallas kernels, on_device(): pl.pallas_call(kernel, out_shape=(jax.ShapeDtypeStruct((1, WIN, WIN, D),...  106 us
    unnamed x7, local copies, waits for them, and re-layouts  3.29 us

profile of v3, /device:TPU:8, one launch (start us, length us, event | category | flops | bytes accessed | tf_op | source)
XLA Modules:
  0.0 109.5 jit_solution(139808127685779337)
XLA Ops:
  0.6 105.5 %window_blocks.1 = (bf16[1,12,12,1024]{3,2,1,0:T(8,128)(2,1)}, f32[16,1024]{1,0:T(8,128)}, f32[16,1024]{1,0:T(8,128)}) custom-call(bf16[1,12,12,1024]{3,2,1,0:T(8,128)(2,1)} %tokens_ref.1, bf16[1,12,12,1024]{3,2,1,0:T(8,128)(2,1)} %grad_ref.1, f32[1,1024]{1,0:T(1,128)} %bitcast.6, f32[1,1024]{1,0:T(1,128)} %bitcast.7, bf16[16,3072]{1,0:T(8,128)(2,1)} %wq1_ref.1, ...), custom_call_target="tpu_custom_call" | custom-call | tf_op jit(solution)/shard_map/window_blocks/pallas_call | solution.py:710
  106.1 0.0 copy-start.1
  106.2 1.8 %copy.18 = bf16[1,12,12,1024]{3,2,1,0:T(8,128)(2,1)} copy(bf16[1,12,12,1024]{3,2,1,0:T(8,128)(2,1)} %get-tuple-element.6) | data formatting | bytes 589824
  108.0 0.0 copy-done.1
  108.0 0.0 copy-start
  108.0 0.6 copy.19
  108.6 0.2 copy-done
  108.8 0.6 copy.20
Async XLA Ops:
  106.1 1.8 %copy-start.1 = (f32[16,1024]{1,0:T(8,128)S(1)}, f32[16,1024]{1,0:T(8,128)}, u32[]{:S(2)}) copy-start(f32[16,1024]{1,0:T(8,128)} %get-tuple-element.7) | copy-start | bytes 196612
  108.0 0.9 copy-start

commit v4 on v3

--- a/solution.py
+++ b/solution.py
@@ -305,7 +305,6 @@
         return jnp.concatenate(
             [rows[c * QUARTER:(c + 1) * QUARTER] for c in range(4)], axis=1)
 
-    roll_out(0, go_f, False)
 
     k_of = iota((TOK, 512), 0)
     lane = iota((TOK, 512), 1)
@@ -594,11 +593,6 @@
     norm_buf[...] = (unit * gain1_ref[...]).astype(BF16)
     g_stack[0, pl.ds(0, TOK), :] = go_f[...].astype(BF16)
     send_grad(0)
-    sh_f[pl.ds(0, QUARTER), :] = go_f[pl.ds(3 * QUARTER, QUARTER), :]
-    for i in range(3):
-        sh_f[pl.ds((i + 1) * QUARTER, QUARTER), :] = roll_in(0, i)
-    g_stack[1, pl.ds(0, TOK), :] = sh_f[...].astype(BF16)
-    send_grad(1)
     gather(5, 0, 1)
     gather(4, 2)
     project(0, True, 0, 1)
@@ -626,6 +620,7 @@
                                   wbuf[3, b, h // 2, h % 2].reshape(BLOCK, BLOCK))
         mid_f[:, cols] = result.astype(BF16).astype(F32)
     roll_out(1, mid_f, False)
+    roll_out(0, go_f, False)
     turn_att(0)
     gather(4, 5, 7)
     gather(4, 6)
@@ -645,6 +640,11 @@
     gather(5, 6)
     project(1, True, 2)
     attend(1, 0, 4)
+    mid_f[pl.ds(0, QUARTER), :] = go_f[pl.ds(3 * QUARTER, QUARTER), :]
+    for i in range(3):
+        mid_f[pl.ds((i + 1) * QUARTER, QUARTER), :] = roll_in(0, i)
+    g_stack[1, pl.ds(0, TOK), :] = mid_f[...].astype(BF16)
+    send_grad(1)
     gather(6, 6)
     project(1, False, 2)
     attend(1, 4, 8)

time: 110 us -> 110 us (level)
  no operation moved by 1% of the time
where the time goes in v4:
time: 110 us
  Pallas kernels  106 us (96%)
  local copies, waits for them, and re-layouts  3.29 us (3%)
    pallas_call x1, Pallas kernels, on_device(): pl.pallas_call(kernel, out_shape=(jax.ShapeDtypeStruct((1, WIN, WIN, D),...  106 us
    unnamed x7, local copies, waits for them, and re-layouts  3.29 us

profile of v4, /device:TPU:8, one launch (start us, length us, event | category | flops | bytes accessed | tf_op | source)
XLA Modules:
  0.0 110.2 jit_solution(2718822612956737077)
XLA Ops:
  0.6 106.3 %window_blocks.1 = (bf16[1,12,12,1024]{3,2,1,0:T(8,128)(2,1)}, f32[16,1024]{1,0:T(8,128)}, f32[16,1024]{1,0:T(8,128)}) custom-call(bf16[1,12,12,1024]{3,2,1,0:T(8,128)(2,1)} %tokens_ref.1, bf16[1,12,12,1024]{3,2,1,0:T(8,128)(2,1)} %grad_ref.1, f32[1,1024]{1,0:T(1,128)} %bitcast.6, f32[1,1024]{1,0:T(1,128)} %bitcast.7, bf16[16,3072]{1,0:T(8,128)(2,1)} %wq1_ref.1, ...), custom_call_target="tpu_custom_call" | custom-call | tf_op jit(solution)/shard_map/window_blocks/pallas_call | solution.py:710
  106.9 0.0 copy-start.1
  106.9 1.8 %copy.18 = bf16[1,12,12,1024]{3,2,1,0:T(8,128)(2,1)} copy(bf16[1,12,12,1024]{3,2,1,0:T(8,128)(2,1)} %get-tuple-element.6) | data formatting | bytes 589824
  108.7 0.0 copy-done.1
  108.7 0.0 copy-start
  108.7 0.6 copy.19
  109.3 0.2 copy-done
  109.6 0.6 copy.20
Async XLA Ops:
  106.9 1.8 %copy-start.1 = (f32[16,1024]{1,0:T(8,128)S(1)}, f32[16,1024]{1,0:T(8,128)}, u32[]{:S(2)}) copy-start(f32[16,1024]{1,0:T(8,128)} %get-tuple-element.7) | copy-start | bytes 196612
  108.7 0.9 copy-start
